TPU v7x, 256 devices: a whole 4x4x8 slice. The times are simulated.
256 devices in a mesh: layer: 8 (over z_lo, y), facet: 32 (over x, z_hi, core).
Axes of the slice: x: 4, y: 4, z: 8 (z_hi: 4, z_lo: 2; z = z_hi * 2 + z_lo), core: 2. Of those that a mesh axis runs over, the one named last changes fastest.
Arguments:
- slabs: bfloat16 [8, 2, 64, 98304], P('layer', None, None, 'facet'), may hold values from -6 to 6
- window: float32 [98304], P('facet'), may hold values from 0.5 to 1.5
- density: int32 [8, 64, 16384], P('layer', None, 'facet'), may hold values from 0 to 7
- offsets: int32 [32], replicated, may hold values from 0 to 98303
Outputs:
- image_out: float32 [2, 64, 98304], P(None, 'layer', 'facet')
All inputs are finite; a program needn't handle non-finite values.
Results may differ from a plain program's by a relative error of at most 0.0052.
Values may be sent and summed in bfloat16 or wider, within the bound.
No kernel may reach another device: no remote copies, remote signals or barrier semaphores. Data moves between devices by JAX's collectives and lax.ppermute only.
A program may use at most 64 MiB of HBM per device.

v0:
```python
import math

import jax
import jax.numpy as jnp
from jax import lax
from jax.sharding import PartitionSpec as P

CONTRIB = 128
SUB = 512


two_pi = 2.0 * math.pi


def mulmod(left_term, right_term, modulus):
    upper_part = right_term // 256
    lower_part = right_term % 256
    return jnp.mod(jnp.mod(left_term * upper_part, modulus) * 256 + left_term * lower_part, modulus)


def phase_parts(first_ints, places, image_width):
    phase_turns = mulmod(first_ints[:, None], places[None, :], image_width)
    phase_angle = phase_turns.astype(jnp.float32) * (-two_pi / image_width)
    return (jnp.cos(phase_angle), jnp.sin(phase_angle))


def embed_table(facet_count, facet_width, contrib_len, sub_len, image_width):
    sample_step = sub_len // contrib_len
    centres = jnp.arange(facet_count, dtype=jnp.int32) * facet_width + facet_width // 2
    sample_pos = jnp.arange(contrib_len, dtype=jnp.int32) * sample_step
    cell_ids = jnp.arange(sub_len, dtype=jnp.int32)
    spacing = cell_ids[None, :] - sample_pos[:, None]
    phase_turns = jnp.mod(spacing[None, :, :] * centres[:, None, None], image_width)
    phase_angle = phase_turns.astype(jnp.float32) * (-two_pi / image_width)
    scaled = spacing.astype(jnp.float32) / sample_step
    kernel = 1.0 / (1.0 + scaled * scaled)
    return jnp.stack([jnp.cos(phase_angle) * kernel, jnp.sin(phase_angle) * kernel], 1).astype(
        jnp.bfloat16
    )


def shards(slabs, window, density, offsets):
    facets = lax.axis_size("facet")
    position = lax.axis_index("facet")
    layer_slab = slabs[0]
    columns = layer_slab.shape[1]
    facet_width = layer_slab.shape[2]
    sample_step = SUB // CONTRIB
    image_width = facet_width * facets
    blocks = facets // 4
    block_ids = jnp.arange(blocks, dtype=jnp.int32)
    x_start = position * facet_width
    windowed = (layer_slab.astype(jnp.float32) * window[None, None, :]).astype(jnp.bfloat16)
    stacked = windowed.reshape(2 * columns, facet_width)
    places = x_start + jnp.arange(facet_width, dtype=jnp.int32)
    offset_cos, offset_sin = phase_parts(jnp.mod(offsets, image_width), places, image_width)
    step_cos, step_sin = phase_parts(
        sample_step * jnp.arange(CONTRIB, dtype=jnp.int32), places, image_width
    )

    def table_for(block_id):
        first_cos = lax.dynamic_slice_in_dim(offset_cos, block_id * 4, 4, 0)[:, None, :]
        first_sin = lax.dynamic_slice_in_dim(offset_sin, block_id * 4, 4, 0)[:, None, :]
        cos_part = first_cos * step_cos[None] - first_sin * step_sin[None]
        sin_part = first_cos * step_sin[None] + first_sin * step_cos[None]
        return jnp.stack([cos_part, sin_part], 1).astype(jnp.bfloat16)

    def encode_block(block_id):
        phase_table = table_for(block_id).reshape(8 * CONTRIB, facet_width)
        product = lax.dot_general(
            stacked, phase_table, (((1,), (1,)), ((), ())), preferred_element_type=jnp.float32
        )
        product = product.reshape(2, columns, 4, 2, CONTRIB)
        real_part = product[0, :, :, 0] - product[1, :, :, 1]
        imag_part = product[0, :, :, 1] + product[1, :, :, 0]
        return jnp.stack([real_part, imag_part], 0)

    pieces = lax.map(encode_block, block_ids)
    outgoing = (
        jnp.transpose(pieces, (0, 3, 1, 2, 4)).reshape(facets, 2, columns, CONTRIB)
        * facet_width ** (-0.5)
    ).astype(jnp.bfloat16)
    received = lax.all_to_all(outgoing, "facet", split_axis=0, concat_axis=0, tiled=True)
    embed_phase = embed_table(facets, facet_width, CONTRIB, SUB, image_width)
    raw_prod = lax.dot_general(
        received, embed_phase, (((0, 3), (0, 2)), ((), ())), preferred_element_type=jnp.float32
    )
    real_part = raw_prod[0, :, 0] - raw_prod[1, :, 1]
    imag_part = raw_prod[0, :, 1] + raw_prod[1, :, 0]
    counts = density[0]
    weights = jnp.where(
        counts > 0,
        1.0 / jnp.maximum(counts, 1).astype(jnp.float32),
        jnp.zeros(counts.shape, jnp.float32),
    )
    gridded = (
        jnp.stack([real_part, imag_part], 0) * weights[None] * (2 * facets) ** (-0.5)
    ).astype(jnp.bfloat16)
    raw_back = lax.dot_general(
        gridded, embed_phase, (((2,), (3,)), ((), ())), preferred_element_type=jnp.float32
    )
    real_back = raw_back[0, :, :, 0] + raw_back[1, :, :, 1]
    imag_back = raw_back[1, :, :, 0] - raw_back[0, :, :, 1]
    back_out = (jnp.stack([real_back, imag_back], 0) * 0.5).astype(jnp.bfloat16)
    returned = lax.all_to_all(back_out, "facet", split_axis=2, concat_axis=2, tiled=True)
    out_scale = (facets * CONTRIB) ** (-0.5)
    row_sets = [returned]
    part_cols = row_sets[0].shape[1]

    def add_block(running, block_id):
        phase_table = table_for(block_id)
        terms = []
        for row_set in row_sets:
            part_rows = lax.dynamic_slice_in_dim(row_set, block_id * 4, 4, 2)
            terms.append(
                lax.dot_general(
                    part_rows,
                    phase_table,
                    (((2, 3), (0, 2)), ((), ())),
                    preferred_element_type=jnp.float32,
                )
            )
        combined = terms[0]
        for extra_term in terms[1:]:
            combined = combined + extra_term
        real_out = combined[0, :, 0] + combined[1, :, 1]
        imag_out = combined[1, :, 0] - combined[0, :, 1]
        return (running + jnp.stack([real_out, imag_out], 0), None)

    running, unused = lax.scan(
        add_block, jnp.zeros((2, part_cols, facet_width), jnp.float32), block_ids
    )
    layer_image = running * window[None, None, :] * out_scale
    image_out = lax.psum_scatter(layer_image, "layer", scatter_dimension=1, tiled=True)
    return image_out


def solution(mesh):
    placed = (P("layer", None, None, "facet"), P("facet"), P("layer", None, "facet"), P())
    return jax.shard_map(
        shards, mesh=mesh, in_specs=placed, out_specs=P(None, "layer", "facet"), check_vma=False
    )
```

profile of v0, /device:TPU:1, one launch (start us, length us, event | category | flops | bytes accessed | tf_op | source)
XLA Modules:
  0.0 413.1 jit_solution(17286400977880995175)
XLA Ops:
  7.8 2.2 fusion.47
  10.0 3.4 fusion.66
  13.9 132.7 %while.25 = (s32[]{:T(128)}, f32[8,2,64,4,128]{4,3,2,1,0:T(4,128)S(1)}, s32[8]{0:T(128)}, f32[32,3072]{1,0:T(8,128)}, f32[32,3072]{1,0:T(8,128)S(1)}, /*index=5*...) while((s32[]{:T(128)}, ...), condition=%wide.region_1.2_spmd.clone.clone, body=%wide.region_0.1_spmd.clone.clone.sunk | while | flops 828243968 | bytes 40166108 | solution.py:78
  16.7 8.0 %fusion.95 = (f32[128,3072]{1,0:T(8,128)S(1)}, f32[128,3072]{1,0:T(8,128)S(1)}) fusion(s32[3072]{0:T(1024)S(1)} %get-tuple-element.500, s32[3072]{0:T(1024)} %get-tuple-element.499, s32[128]{0:T(128)S(1)} %get-tuple-element.501), kind=kLoop, calls=%fused_computation.20.clone.1 | loop fusion | flops 7077888 | bytes 3170816 | tf_op jit(solution)/shard_map/cos | solution.py:24
  24.7 1.8 subtract_convert_fusion.4
  27.5 1.8 convolution_bitcast_fusion.2
  33.2 8.0 %fusion.95 = (f32[128,3072]{1,0:T(8,128)S(1)}, f32[128,3072]{1,0:T(8,128)S(1)}) fusion(s32[3072]{0:T(1024)S(1)} %get-tuple-element.500, s32[3072]{0:T(1024)} %get-tuple-element.499, s32[128]{0:T(128)S(1)} %get-tuple-element.501), kind=kLoop, calls=%fused_computation.20.clone.1 | loop fusion | flops 7077888 | bytes 3170816 | tf_op jit(solution)/shard_map/cos | solution.py:24
  41.2 1.8 subtract_convert_fusion.4
  44.1 1.8 convolution_bitcast_fusion.2
  49.8 8.0 %fusion.95 = (f32[128,3072]{1,0:T(8,128)S(1)}, f32[128,3072]{1,0:T(8,128)S(1)}) fusion(s32[3072]{0:T(1024)S(1)} %get-tuple-element.500, s32[3072]{0:T(1024)} %get-tuple-element.499, s32[128]{0:T(128)S(1)} %get-tuple-element.501), kind=kLoop, calls=%fused_computation.20.clone.1 | loop fusion | flops 7077888 | bytes 3170816 | tf_op jit(solution)/shard_map/cos | solution.py:24
  57.8 1.8 subtract_convert_fusion.4
  60.7 1.8 convolution_bitcast_fusion.2
  66.4 8.0 %fusion.95 = (f32[128,3072]{1,0:T(8,128)S(1)}, f32[128,3072]{1,0:T(8,128)S(1)}) fusion(s32[3072]{0:T(1024)S(1)} %get-tuple-element.500, s32[3072]{0:T(1024)} %get-tuple-element.499, s32[128]{0:T(128)S(1)} %get-tuple-element.501), kind=kLoop, calls=%fused_computation.20.clone.1 | loop fusion | flops 7077888 | bytes 3170816 | tf_op jit(solution)/shard_map/cos | solution.py:24
  74.3 1.8 subtract_convert_fusion.4
  77.2 1.8 convolution_bitcast_fusion.2
  82.9 8.0 %fusion.95 = (f32[128,3072]{1,0:T(8,128)S(1)}, f32[128,3072]{1,0:T(8,128)S(1)}) fusion(s32[3072]{0:T(1024)S(1)} %get-tuple-element.500, s32[3072]{0:T(1024)} %get-tuple-element.499, s32[128]{0:T(128)S(1)} %get-tuple-element.501), kind=kLoop, calls=%fused_computation.20.clone.1 | loop fusion | flops 7077888 | bytes 3170816 | tf_op jit(solution)/shard_map/cos | solution.py:24
  90.9 1.8 subtract_convert_fusion.4
  93.8 1.8 convolution_bitcast_fusion.2
  99.5 8.0 %fusion.95 = (f32[128,3072]{1,0:T(8,128)S(1)}, f32[128,3072]{1,0:T(8,128)S(1)}) fusion(s32[3072]{0:T(1024)S(1)} %get-tuple-element.500, s32[3072]{0:T(1024)} %get-tuple-element.499, s32[128]{0:T(128)S(1)} %get-tuple-element.501), kind=kLoop, calls=%fused_computation.20.clone.1 | loop fusion | flops 7077888 | bytes 3170816 | tf_op jit(solution)/shard_map/cos | solution.py:24
  107.5 1.8 subtract_convert_fusion.4
  110.4 1.8 convolution_bitcast_fusion.2
  116.1 8.0 %fusion.95 = (f32[128,3072]{1,0:T(8,128)S(1)}, f32[128,3072]{1,0:T(8,128)S(1)}) fusion(s32[3072]{0:T(1024)S(1)} %get-tuple-element.500, s32[3072]{0:T(1024)} %get-tuple-element.499, s32[128]{0:T(128)S(1)} %get-tuple-element.501), kind=kLoop, calls=%fused_computation.20.clone.1 | loop fusion | flops 7077888 | bytes 3170816 | tf_op jit(solution)/shard_map/cos | solution.py:24
  124.0 1.8 subtract_convert_fusion.4
  126.9 1.8 convolution_bitcast_fusion.2
  132.6 8.0 %fusion.95 = (f32[128,3072]{1,0:T(8,128)S(1)}, f32[128,3072]{1,0:T(8,128)S(1)}) fusion(s32[3072]{0:T(1024)S(1)} %get-tuple-element.500, s32[3072]{0:T(1024)} %get-tuple-element.499, s32[128]{0:T(128)S(1)} %get-tuple-element.501), kind=kLoop, calls=%fused_computation.20.clone.1 | loop fusion | flops 7077888 | bytes 3170816 | tf_op jit(solution)/shard_map/cos | solution.py:24
  140.6 1.8 subtract_convert_fusion.4
  143.5 1.8 convolution_bitcast_fusion.2
  147.2 1.3 copy.23
  148.5 12.6 %all-to-all-start = ((bf16[32,2,64,128]{3,2,1,0:T(8,128)(2,1)}), bf16[32,2,64,128]{3,2,1,0:T(8,128)(2,1)S(1)}, u32[]{:S(2)}, u32[]{:S(2)}) async-start(bf16[32,2,64,128]{3,2,1,0:T(8,128)(2,1)} %bitcast.2), calls=%async_computation | async-start | bytes 2097152 | tf_op jit(solution)/shard_map/all_to_all | solution.py:83
  161.4 36.6 %multiply_convert_fusion.1 = (bf16[32,1,128,512]{3,2,0,1:T(8,128)(2,1)}, bf16[32,1,128,512]{3,2,0,1:T(8,128)(2,1)}) fusion(f32[128,512]{1,0:T(8,128)S(1)} %add_divide_fusion, s32[32]{0:T(128)S(1)} %multiply_add_fusion, s32[128,512]{1,0:T(8,128)S(1)} %iota_subtract_fusion), kind=kLoop, calls=%fused_computation.67 | loop fusion | flops 27262976 | bytes 8913024 | tf_op jit(solution)/shard_map/convert.5
  198.0 4.4 %fusion.48 = f32[2,64,2,512]{3,1,2,0:T(8,128)S(1)} fusion(bf16[32,1,128,512]{3,2,0,1:T(8,128)(2,1)} %get-tuple-element.316, bf16[32,1,128,512]{3,2,0,1:T(8,128)(2,1)} %get-tuple-element.315, bf16[32,2,64,128]{3,2,1,0:T(8,128)(2,1)S(1)} %all-to-all-done), kind=kOutput, calls=%fused_computation.78 | convolution fusion | flops 1090519040 | bytes 9961472 | tf_op jit(solution)/shard_map/dot_general | solution.py:85
  202.6 1.3 copy-done.1
  203.9 2.8 fusion.38
  208.4 9.8 %all-to-all-start.1 = ((bf16[2,64,32,128]{3,1,0,2:T(8,128)(2,1)}), bf16[2,64,32,128]{3,1,0,2:T(8,128)(2,1)}, u32[]{:S(2)}, u32[]{:S(2)}) async-start(bf16[2,64,32,128]{3,1,0,2:T(8,128)(2,1)} %copy.28), calls=%async_computation.1 | async-start | bytes 2097152 | tf_op jit(solution)/shard_map/all_to_all | solution.py:105
  218.3 28.1 %all-to-all-done.1 = bf16[2,64,32,128]{3,1,0,2:T(8,128)(2,1)} async-done(((bf16[2,64,32,128]{3,1,0,2:T(8,128)(2,1)}), bf16[2,64,32,128]{3,1,0,2:T(8,128)(2,1)}, u32[]{:S(2)}, u32[]{:S(2)}) %all-to-all-start.1) | async-done | bytes 1048608 | tf_op jit(solution)/shard_map/all_to_all | solution.py:105
  246.9 121.3 %while.26 = (s32[]{:T(128)}, f32[2,64,3072]{2,1,0:T(8,128)S(1)}, s32[8]{0:T(128)}, bf16[2,64,32,128]{3,1,0,2:T(8,128)(2,1)}, f32[32,3072]{1,0:T(8,128)}, /*index...) while((s32[]{:T(128)}, f32[2,64,3072]{2,1,0:T(8,128)S(1)}, ...), condition=%wide.region_3.4_spmd.clone.clone.clone, body=%wide.region_2.3_spmd.clone.clone.clone.sunk | while | flops 839122944 | bytes 31908552 | solution.py:130
  249.7 8.0 %fusion.98 = (f32[128,3072]{1,0:T(8,128)S(1)}, f32[128,3072]{1,0:T(8,128)S(1)}) fusion(s32[3072]{0:T(1024)S(1)} %get-tuple-element.539, s32[3072]{0:T(1024)} %get-tuple-element.538, s32[128]{0:T(128)S(1)} %get-tuple-element.540), kind=kLoop, calls=%fused_computation.51.clone.1 | loop fusion | flops 7077888 | bytes 3170816 | tf_op jit(solution)/shard_map/cos | solution.py:24
  257.7 1.7 subtract_convert_fusion.5
  259.4 1.9 fusion.99
  262.1 1.3 dynamic_slice.56
  264.9 8.0 %fusion.98 = (f32[128,3072]{1,0:T(8,128)S(1)}, f32[128,3072]{1,0:T(8,128)S(1)}) fusion(s32[3072]{0:T(1024)S(1)} %get-tuple-element.539, s32[3072]{0:T(1024)} %get-tuple-element.538, s32[128]{0:T(128)S(1)} %get-tuple-element.540), kind=kLoop, calls=%fused_computation.51.clone.1 | loop fusion | flops 7077888 | bytes 3170816 | tf_op jit(solution)/shard_map/cos | solution.py:24
  272.9 1.7 subtract_convert_fusion.5
  274.6 1.9 fusion.99
  277.2 1.3 dynamic_slice.56
  280.0 8.0 %fusion.98 = (f32[128,3072]{1,0:T(8,128)S(1)}, f32[128,3072]{1,0:T(8,128)S(1)}) fusion(s32[3072]{0:T(1024)S(1)} %get-tuple-element.539, s32[3072]{0:T(1024)} %get-tuple-element.538, s32[128]{0:T(128)S(1)} %get-tuple-element.540), kind=kLoop, calls=%fused_computation.51.clone.1 | loop fusion | flops 7077888 | bytes 3170816 | tf_op jit(solution)/shard_map/cos | solution.py:24
  288.0 1.7 subtract_convert_fusion.5
  289.7 1.9 fusion.99
  295.2 8.0 %fusion.98 = (f32[128,3072]{1,0:T(8,128)S(1)}, f32[128,3072]{1,0:T(8,128)S(1)}) fusion(s32[3072]{0:T(1024)S(1)} %get-tuple-element.539, s32[3072]{0:T(1024)} %get-tuple-element.538, s32[128]{0:T(128)S(1)} %get-tuple-element.540), kind=kLoop, calls=%fused_computation.51.clone.1 | loop fusion | flops 7077888 | bytes 3170816 | tf_op jit(solution)/shard_map/cos | solution.py:24
  303.2 1.7 subtract_convert_fusion.5
  304.9 1.9 fusion.99
  310.4 8.0 %fusion.98 = (f32[128,3072]{1,0:T(8,128)S(1)}, f32[128,3072]{1,0:T(8,128)S(1)}) fusion(s32[3072]{0:T(1024)S(1)} %get-tuple-element.539, s32[3072]{0:T(1024)} %get-tuple-element.538, s32[128]{0:T(128)S(1)} %get-tuple-element.540), kind=kLoop, calls=%fused_computation.51.clone.1 | loop fusion | flops 7077888 | bytes 3170816 | tf_op jit(solution)/shard_map/cos | solution.py:24
  318.4 1.7 subtract_convert_fusion.5
  320.1 1.9 fusion.99
  325.5 8.0 %fusion.98 = (f32[128,3072]{1,0:T(8,128)S(1)}, f32[128,3072]{1,0:T(8,128)S(1)}) fusion(s32[3072]{0:T(1024)S(1)} %get-tuple-element.539, s32[3072]{0:T(1024)} %get-tuple-element.538, s32[128]{0:T(128)S(1)} %get-tuple-element.540), kind=kLoop, calls=%fused_computation.51.clone.1 | loop fusion | flops 7077888 | bytes 3170816 | tf_op jit(solution)/shard_map/cos | solution.py:24
  333.5 1.7 subtract_convert_fusion.5
  335.2 1.9 fusion.99
  340.7 8.0 %fusion.98 = (f32[128,3072]{1,0:T(8,128)S(1)}, f32[128,3072]{1,0:T(8,128)S(1)}) fusion(s32[3072]{0:T(1024)S(1)} %get-tuple-element.539, s32[3072]{0:T(1024)} %get-tuple-element.538, s32[128]{0:T(128)S(1)} %get-tuple-element.540), kind=kLoop, calls=%fused_computation.51.clone.1 | loop fusion | flops 7077888 | bytes 3170816 | tf_op jit(solution)/shard_map/cos | solution.py:24
  348.7 1.7 subtract_convert_fusion.5
  350.4 1.9 fusion.99
  355.9 8.0 %fusion.98 = (f32[128,3072]{1,0:T(8,128)S(1)}, f32[128,3072]{1,0:T(8,128)S(1)}) fusion(s32[3072]{0:T(1024)S(1)} %get-tuple-element.539, s32[3072]{0:T(1024)} %get-tuple-element.538, s32[128]{0:T(128)S(1)} %get-tuple-element.540), kind=kLoop, calls=%fused_computation.51.clone.1 | loop fusion | flops 7077888 | bytes 3170816 | tf_op jit(solution)/shard_map/cos | solution.py:24
  363.8 1.7 subtract_convert_fusion.5
  365.6 1.9 fusion.99
  368.2 2.0 multiply_multiply_fusion
  370.2 36.0 %reduce-scatter.2.cloned.1.call-done = f32[2,8,3072]{2,1,0:T(8,128)} async-done(((f32[2,64,3072]{2,1,0:T(8,128)}), f32[2,8,3072]{2,1,0:T(8,128)}) %reduce-scatter.2.cloned.1.call-update) | async-done | bytes 196624 | tf_op jit(solution)/shard_map/reduce_scatter | solution.py:134
  (135 shorter events, 60.3 us)
Async XLA Ops:
  26.4 1.1 copy-start.2
  43.0 1.1 copy-start.2
  59.5 1.1 copy-start.2
  76.1 1.1 copy-start.2
  92.7 1.1 copy-start.2
  109.2 1.1 copy-start.2
  125.8 1.1 copy-start.2
  142.4 1.1 copy-start.2
  146.6 14.5 %copy-start.3 = (s32[1,64,512]{2,1,0:T(8,128)S(1)}, s32[1,64,512]{2,1,0:T(8,128)}, u32[]{:S(2)}) copy-start(s32[1,64,512]{2,1,0:T(8,128)} %param.10) | copy-start | bytes 393220
  148.5 49.5 %all-to-all-start = ((bf16[32,2,64,128]{3,2,1,0:T(8,128)(2,1)}), bf16[32,2,64,128]{3,2,1,0:T(8,128)(2,1)S(1)}, u32[]{:S(2)}, u32[]{:S(2)}) async-start(bf16[32,2,64,128]{3,2,1,0:T(8,128)(2,1)} %bitcast.2), calls=%async_computation | async-start | bytes 2097152 | tf_op jit(solution)/shard_map/all_to_all | solution.py:83
  198.0 4.7 %copy-start = (bf16[32,1,128,512]{3,2,0,1:T(8,128)(2,1)S(1)}, bf16[32,1,128,512]{3,2,0,1:T(8,128)(2,1)}, u32[]{:S(2)}) copy-start(bf16[32,1,128,512]{3,2,0,1:T(8,128)(2,1)} %get-tuple-element.315) | copy-start | bytes 12582916
  198.0 5.9 %copy-start.1 = (bf16[32,1,128,512]{3,2,0,1:T(8,128)(2,1)S(1)}, bf16[32,1,128,512]{3,2,0,1:T(8,128)(2,1)}, u32[]{:S(2)}) copy-start(bf16[32,1,128,512]{3,2,0,1:T(8,128)(2,1)} %get-tuple-element.316) | copy-start | bytes 12582916
  208.4 38.0 %all-to-all-start.1 = ((bf16[2,64,32,128]{3,1,0,2:T(8,128)(2,1)}), bf16[2,64,32,128]{3,1,0,2:T(8,128)(2,1)}, u32[]{:S(2)}, u32[]{:S(2)}) async-start(bf16[2,64,32,128]{3,1,0,2:T(8,128)(2,1)} %copy.28), calls=%async_computation.1 | async-start | bytes 2097152 | tf_op jit(solution)/shard_map/all_to_all | solution.py:105
  218.2 188.0 %reduce-scatter.2.cloned.1.call-start = ((), (), s32[]{:S(2)}) async-start(), calls=%async_computation.3 | async-start | bytes 1769472 | tf_op jit(solution)/shard_map/reduce_scatter | solution.py:134
Sparse Core Ops, SparseCore 0:
  370.3 35.8 reduce-scatter.1
where the time goes:
time: 420 us; the launch traced here: 413 us
  other arithmetic  216 us (51%)
  waiting for transfers between devices  64.1 us (15%)
  local copies, waits for them, and re-layouts  49.1 us (12%)
  matrix products  36.6 us (9%)
  starting transfers between devices  22.5 us (5%)
  between operations  13.5 us (3%)
  loops' own time  11.5 us (3%)
    cos x16, other arithmetic, phase_parts(): return (jnp.cos(phase_angle), jnp.sin(phase_angle))  128 us
    another operation x17, other arithmetic  64.3 us
    reduce_scatter x1, waiting for transfers between devices, shards(): lax.psum_scatter(layer_image, 'layer', scatter_dimension=1, tiled=True)  36 us
    all_to_all x1, waiting for transfers between devices, shards(): lax.all_to_all(back_out, 'facet', split_axis=2, concat_axis=2, tiled=True)  28.1 us
    dynamic_slice x16, local copies, waits for them, and re-layouts, shards(): pieces = lax.map(encode_block, block_ids)  19.9 us
    dot_general x8, matrix products, add_block(): lax.dot_general(part_rows, phase_table, (((2, 3), (0, 2)), ((), ())), pre...  15.2 us
    dynamic_slice x16, local copies, waits for them, and re-layouts, table_for(): lax.dynamic_slice_in_dim(offset_sin, block_id * 4, 4, 0)[:, None, :]  14.7 us
    dot_general x8, matrix products, encode_block(): lax.dot_general(stacked, phase_table, (((1,), (1,)), ((), ())), preferred...  14.3 us
  transfers between devices with their start and end apart: 3, of which 2 were waited for; matrix products, arithmetic and copies ran while one was open for 9% of the time, Pallas kernels for 0%

commit v1 on v0

v1 whole, which is shorter than its diff:
```python
import math

import jax
import jax.numpy as jnp
import ml_dtypes
import numpy as np
from jax import lax
from jax.experimental import pallas as pl
from jax.experimental.pallas import tpu as pltpu
from jax.sharding import PartitionSpec as P

CONTRIB = 128
SUB = 512
LANES = 128
GROUP = 4

two_pi = 2.0 * math.pi
NT = (((1,), (1,)), ((), ()))
NN = (((1,), (0,)), ((), ()))


def mulmod(left_term, right_term, modulus):
    upper_part = right_term // 256
    lower_part = right_term % 256
    return jnp.mod(jnp.mod(left_term * upper_part, modulus) * 256 + left_term * lower_part, modulus)


def offset_phases(offsets, places, image_width):
    phase_turns = mulmod(offsets[:, None], places[None, :], image_width)
    phase_angle = phase_turns.astype(jnp.float32) * (two_pi / image_width)
    return jnp.cos(phase_angle), jnp.sin(phase_angle)


def step_table(facet_width, image_width, sample_step):
    j = np.arange(CONTRIB, dtype=np.int64)[:, None]
    cell = np.arange(facet_width, dtype=np.int64)[None, :] - facet_width // 2
    angle = np.mod(sample_step * j * cell, image_width) * (-2.0 * np.pi / image_width)
    return np.concatenate([np.cos(angle), np.sin(angle)], 0).astype(ml_dtypes.bfloat16)


def kernel_table(sample_step):
    spacing = np.arange(SUB)[None, :] - sample_step * np.arange(CONTRIB)[:, None]
    scaled = spacing / sample_step
    return (1.0 / (1.0 + scaled * scaled)).astype(ml_dtypes.bfloat16)


def centre_phases(facets):
    turns = np.mod(
        np.arange(SUB)[None, :] * (2 * np.arange(facets)[:, None] + 1), 2 * facets
    )
    angle = turns * (np.pi / facets)
    return np.cos(angle).astype(np.float32), np.sin(angle).astype(np.float32)


def fill_phases(hc_ref, hs_ref, lc_ref, ls_ref, pr_ref, pi_ref):
    lc, ls = lc_ref[...], ls_ref[...]
    for tile in range(pr_ref.shape[1] // LANES):
        hc = hc_ref[:, tile : tile + 1]
        hs = hs_ref[:, tile : tile + 1]
        span = slice(tile * LANES, (tile + 1) * LANES)
        pr_ref[:, span] = hc * lc - hs * ls
        pi_ref[:, span] = hs * lc + hc * ls


def encode_kernel(
    slab_ref, window_ref, hc_ref, hs_ref, lc_ref, ls_ref, table_ref, out_ref, w_ref, pr_ref, pi_ref
):
    columns = slab_ref.shape[0] // 2
    width = slab_ref.shape[1]
    step = pl.program_id(0)

    @pl.when(step == 0)
    def _():
        fill_phases(hc_ref, hs_ref, lc_ref, ls_ref, pr_ref, pi_ref)
        for tile in range(width // 256):
            span = slice(tile * 256, (tile + 1) * 256)
            windowed = slab_ref[:, span].astype(jnp.float32) * window_ref[:, span]
            w_ref[:, span] = windowed.astype(jnp.bfloat16).astype(jnp.float32)

    total = None
    for tile in range(width // 256):
        span = slice(tile * 256, (tile + 1) * 256)
        wr = w_ref[0:columns, span]
        wi = w_ref[columns : 2 * columns, span]
        rows = []
        for k in range(GROUP):
            pr = pr_ref[pl.ds(step * GROUP + k, 1), span]
            pi = pi_ref[pl.ds(step * GROUP + k, 1), span]
            rows.append((pr * wr + pi * wi).astype(jnp.bfloat16))
            rows.append((pr * wi - pi * wr).astype(jnp.bfloat16))
        part = lax.dot_general(
            jnp.concatenate(rows, 0), table_ref[:, span], NT, preferred_element_type=jnp.float32
        )
        total = part if total is None else total + part
    scale = width ** (-0.5)
    for k in range(GROUP):
        base = 2 * columns * k
        upper = total[base : base + columns]
        lower = total[base + columns : base + 2 * columns]
        out_ref[k, 0:columns, :] = (
            (upper[:, :CONTRIB] - lower[:, CONTRIB:]) * scale
        ).astype(jnp.bfloat16)
        out_ref[k, columns : 2 * columns, :] = (
            (upper[:, CONTRIB:] + lower[:, :CONTRIB]) * scale
        ).astype(jnp.bfloat16)


def grid_kernel(recv_ref, kernel_ref, cos_ref, sin_ref, counts_ref, out_ref, re_ref, im_ref):
    facets = recv_ref.shape[0]
    columns = recv_ref.shape[1] // 2
    re_ref[...] = jnp.zeros_like(re_ref)
    im_ref[...] = jnp.zeros_like(im_ref)

    def body(block, carry):
        re, im = None, None
        for k in range(4):
            f = block * 4 + k
            spread = lax.dot_general(
                recv_ref[f], kernel_ref[...], NN, preferred_element_type=jnp.float32
            )
            c = cos_ref[pl.ds(f, 1), :]
            s = sin_ref[pl.ds(f, 1), :]
            a, b = spread[:columns], spread[columns:]
            re_term = a * c + b * s
            im_term = b * c - a * s
            re = re_term if re is None else re + re_term
            im = im_term if im is None else im + im_term
        re_ref[...] += re
        im_ref[...] += im
        return carry

    lax.fori_loop(0, facets // 4, body, 0)
    counts = counts_ref[...]
    weights = jnp.where(
        counts > 0, 1.0 / jnp.maximum(counts, 1).astype(jnp.float32), 0.0
    ) * ((2 * facets) ** (-0.5))
    re = re_ref[...] * weights
    im = im_ref[...] * weights
    per = out_ref.shape[1] // 2
    for layer in range(out_ref.shape[0]):
        span = slice(layer * per, (layer + 1) * per)
        out_ref[layer] = jnp.concatenate([re[span], im[span]], 0).astype(jnp.bfloat16)


def back_kernel(recv_ref, kernel_ref, cos_ref, sin_ref, out_ref, rows_ref):
    layers = recv_ref.shape[0]
    facets = out_ref.shape[0]
    total = recv_ref[0].astype(jnp.float32)
    for layer in range(1, layers):
        total = total + recv_ref[layer].astype(jnp.float32)
    per = total.shape[0] // 2
    re, im = total[:per], total[per:]
    for f in range(facets):
        c = cos_ref[f : f + 1, :]
        s = sin_ref[f : f + 1, :]
        turned = jnp.concatenate([re * c - im * s, im * c + re * s], 0)
        rows_ref[f * 2 * per : (f + 1) * 2 * per, :] = turned.astype(jnp.bfloat16)
    back = lax.dot_general(
        rows_ref[...], kernel_ref[...], NT, preferred_element_type=jnp.float32
    )
    out_ref[...] = (back * 0.5).astype(jnp.bfloat16).reshape(out_ref.shape)


def decode_kernel(
    recv_ref, window_ref, hc_ref, hs_ref, lc_ref, ls_ref, table_ref, out_ref, pr_ref, pi_ref
):
    subgrids = recv_ref.shape[0]
    per = recv_ref.shape[1] // 2
    width = out_ref.shape[2]
    fill_phases(hc_ref, hs_ref, lc_ref, ls_ref, pr_ref, pi_ref)
    rows = recv_ref[...].astype(jnp.float32)
    re, im = rows[:, :per], rows[:, per:]
    left_re = jnp.concatenate([re, im], 2).reshape(subgrids * per, 2 * CONTRIB).astype(jnp.bfloat16)
    left_im = jnp.concatenate([im, -re], 2).reshape(subgrids * per, 2 * CONTRIB).astype(jnp.bfloat16)
    scale = (subgrids * CONTRIB) ** (-0.5)
    for tile in range(width // 256):
        span = slice(tile * 256, (tile + 1) * 256)
        table = table_ref[:, span]
        zr = lax.dot_general(left_re, table, NN, preferred_element_type=jnp.float32)
        zi = lax.dot_general(left_im, table, NN, preferred_element_type=jnp.float32)
        out_re, out_im = None, None
        for s in range(subgrids):
            a = zr[s * per : (s + 1) * per]
            b = zi[s * per : (s + 1) * per]
            pr = pr_ref[s : s + 1, span]
            pi = pi_ref[s : s + 1, span]
            re_term = pr * a - pi * b
            im_term = pr * b + pi * a
            out_re = re_term if out_re is None else out_re + re_term
            out_im = im_term if out_im is None else out_im + im_term
        taper = window_ref[:, span] * scale
        out_ref[0, :, span] = out_re * taper
        out_ref[1, :, span] = out_im * taper


def params(**more):
    return pltpu.CompilerParams(vmem_limit_bytes=48 * 2**20, **more)


def shards(slabs, window, density, offsets):
    layers = lax.axis_size("layer")
    facets = lax.axis_size("facet")
    position = lax.axis_index("facet")
    columns, width = slabs.shape[2], slabs.shape[3]
    per = columns // layers
    sample_step = SUB // CONTRIB
    image_width = width * facets
    tiles = width // LANES
    table = jnp.asarray(step_table(width, image_width, sample_step))
    spread = jnp.asarray(kernel_table(sample_step))
    cos_u, sin_u = (jnp.asarray(part) for part in centre_phases(facets))

    residues = jnp.mod(offsets, image_width)
    starts = position * width + LANES * jnp.arange(tiles, dtype=jnp.int32)
    hc, hs = offset_phases(residues, starts, image_width)
    lc, ls = offset_phases(residues, jnp.arange(LANES, dtype=jnp.int32), image_width)
    window_row = window.reshape(1, width)

    whole = pl.BlockSpec(memory_space=pltpu.VMEM)
    outgoing = pl.pallas_call(
        encode_kernel,
        grid=(facets // GROUP,),
        out_shape=jax.ShapeDtypeStruct((facets, 2 * columns, CONTRIB), jnp.bfloat16),
        in_specs=[whole] * 7,
        out_specs=pl.BlockSpec((GROUP, 2 * columns, CONTRIB), lambda g: (g, 0, 0)),
        scratch_shapes=[
            pltpu.VMEM((2 * columns, width), jnp.float32),
            pltpu.VMEM((facets, width), jnp.float32),
            pltpu.VMEM((facets, width), jnp.float32),
        ],
        compiler_params=params(),
        name="encode",
    )(slabs.reshape(2 * columns, width), window_row, hc, hs, lc, ls, table)

    received = lax.all_to_all(outgoing, "facet", split_axis=0, concat_axis=0, tiled=True)

    gridded = pl.pallas_call(
        grid_kernel,
        out_shape=jax.ShapeDtypeStruct((layers, 2 * per, SUB), jnp.bfloat16),
        in_specs=[whole] * 5,
        out_specs=whole,
        scratch_shapes=[pltpu.VMEM((columns, SUB), jnp.float32)] * 2,
        compiler_params=params(),
        name="subgrid",
    )(received, spread, cos_u, sin_u, density[0])

    by_layer = lax.all_to_all(gridded, "layer", split_axis=0, concat_axis=0, tiled=True)

    back_out = pl.pallas_call(
        back_kernel,
        out_shape=jax.ShapeDtypeStruct((facets, 2 * per, CONTRIB), jnp.bfloat16),
        in_specs=[whole] * 4,
        out_specs=whole,
        scratch_shapes=[pltpu.VMEM((facets * 2 * per, SUB), jnp.bfloat16)],
        compiler_params=params(),
        name="back",
    )(by_layer, spread, cos_u, sin_u)

    returned = lax.all_to_all(back_out, "facet", split_axis=0, concat_axis=0, tiled=True)

    return pl.pallas_call(
        decode_kernel,
        out_shape=jax.ShapeDtypeStruct((2, per, width), jnp.float32),
        in_specs=[whole] * 7,
        out_specs=whole,
        scratch_shapes=[pltpu.VMEM((facets, width), jnp.float32)] * 2,
        compiler_params=params(),
        name="decode",
    )(returned, window_row, hc, hs, lc, ls, table)


def solution(mesh):
    placed = (P("layer", None, None, "facet"), P("facet"), P("layer", None, "facet"), P())
    return jax.shard_map(
        shards, mesh=mesh, in_specs=placed, out_specs=P(None, "layer", "facet"), check_vma=False
    )
```

time: 420 us -> 87.3 us (0.21); the launches traced: 413 us -> 87 us
  other arithmetic: 216 us -> 1.02 us
  blocking collectives: 0 us -> 67.9 us
  waiting for transfers between devices: 64.1 us -> 0 us
  local copies, waits for them, and re-layouts: 49.1 us -> 3.28 us
  matrix products: 36.6 us -> 0 us
  starting transfers between devices: 22.5 us -> 0 us
  Pallas kernels: 0 us -> 14.7 us
  between operations: 13.5 us -> 0.09 us
  loops' own time: 11.5 us -> 0 us
    cos x16 -> x0, other arithmetic: 128 us -> none  [phase_parts(): return (jnp.cos(phase_angle), jnp.sin(phase_angle))]
    another operation x25 -> x0, other arithmetic: 68.9 us -> none
    all_to_all x0 -> x3, blocking collectives: none -> 67.9 us  [the longest x1 40.6 us: shards(): lax.all_to_all(outgoing, 'facet', split_axis=0, concat_axis=0, tiled=True)]
    dot_general x18 -> x0, matrix products: 36.6 us -> none  [the longest x8 15.2 us: add_block(): lax.dot_general(part_rows, phase_table, (((2, 3), (0, 2)), ((), ())), pre...]
    reduce_scatter x1 -> x0, waiting for transfers between devices: 36 us -> none  [shards(): lax.psum_scatter(layer_image, 'layer', scatter_dimension=1, tiled=True)]
    dynamic_slice x32 -> x0, local copies, waits for them, and re-layouts: 34.6 us -> none  [the longest x16 19.9 us: shards(): pieces = lax.map(encode_block, block_ids)]
    all_to_all x2 -> x0, waiting for transfers between devices: 28.1 us -> none  [the longest x1 28.1 us: shards(): lax.all_to_all(back_out, 'facet', split_axis=2, concat_axis=2, tiled=True)]
    all_to_all x2 -> x0, starting transfers between devices: 22.4 us -> none  [the longest x1 12.6 us: shards(): lax.all_to_all(outgoing, 'facet', split_axis=0, concat_axis=0, tiled=True)]
  transfers between devices with their start and end apart: 3 -> 0, of which waited for: 2 -> 0; matrix products, arithmetic and copies ran while one was open for 9% -> 0% of each run, Pallas kernels for 0% -> 0%
where the time goes in v1:
time: 87.3 us; the launch traced here: 87 us
  blocking collectives  67.9 us (78%)
  Pallas kernels  14.7 us (17%)
  local copies, waits for them, and re-layouts  3.28 us (4%)
  other arithmetic  1.02 us (1%)
    all_to_all x1, blocking collectives, shards(): lax.all_to_all(outgoing, 'facet', split_axis=0, concat_axis=0, tiled=True)  40.6 us
    all_to_all x1, blocking collectives, shards(): lax.all_to_all(back_out, 'facet', split_axis=0, concat_axis=0, tiled=True)  16.1 us
    all_to_all x1, blocking collectives, shards(): lax.all_to_all(gridded, 'layer', split_axis=0, concat_axis=0, tiled=True)  11.2 us
    pallas_call x1, Pallas kernels, shards(): pl.pallas_call(encode_kernel, grid=(facets // GROUP,), out_shape=jax.Shap...  9.68 us
    unnamed x18, local copies, waits for them, and re-layouts  3.28 us
    pallas_call x1, Pallas kernels, shards(): pl.pallas_call(grid_kernel, out_shape=jax.ShapeDtypeStruct((layers, 2 * p...  2.69 us
    pallas_call x1, Pallas kernels, shards(): pl.pallas_call(decode_kernel, out_shape=jax.ShapeDtypeStruct((2, per, wid...  2.02 us

profile of v1, /device:TPU:1, one launch (start us, length us, event | category | flops | bytes accessed | tf_op | source)
XLA Modules:
  0.0 87.0 jit_solution(10738485599041670356)
XLA Ops:
  0.0 0.7 and_select_fusion.4
  0.7 0.2 fusion.16
  0.9 0.2 fusion.18
  1.0 0.0 copy-start
  1.0 1.4 %copy-done = bf16[256,3072]{1,0:T(8,128)(2,1)S(1)} copy-done((bf16[256,3072]{1,0:T(8,128)(2,1)S(1)}, bf16[256,3072]{1,0:T(8,128)(2,1)}, u32[]{:S(2)}) %copy-start) | copy-done | bytes 1572888
  2.4 0.0 copy-start.2
  2.4 1.1 %copy-done.2 = bf16[1,2,64,3072]{3,2,1,0:T(8,128)(2,1)S(1)} copy-done((bf16[1,2,64,3072]{3,2,1,0:T(8,128)(2,1)S(1)}, bf16[1,2,64,3072]{3,2,1,0:T(8,128)(2,1)}, u32[]{:S(2)}) %copy-start.2) | copy-done | bytes 786456
  3.6 0.0 copy-start.7
  3.6 0.7 copy-done.7
  4.3 9.7 %encode.1 = bf16[32,128,128]{2,1,0:T(8,128)(2,1)S(1)} custom-call(bf16[128,3072]{1,0:T(8,128)(2,1)S(1)} %bitcast.3, f32[1,3072]{1,0:T(1,128)S(1)} %bitcast.5, f32[32,24]{1,0:T(8,128)S(1)} %get-tuple-element.8.hc_ref, f32[32,24]{1,0:T(8,128)S(1)} %get-tuple-element.7.hs_ref, f32[32,128]{1,0:T(8,128)S(1)} %get-tuple-element.6.lc_ref, ...), custom_call_target="tpu_custom_call" | custom-call | tf_op jit(solution)/shard_map/encode/pallas_call | solution.py:220
  14.0 0.0 copy-start.3
  14.0 0.0 copy-start.4
  14.0 0.0 copy-start.5
  14.0 0.0 copy-start.6
  14.0 40.6 %all_to_all.15.recv_ref = bf16[32,128,128]{2,1,0:T(8,128)(2,1)S(1)} all-to-all(bf16[32,128,128]{2,1,0:T(8,128)(2,1)S(1)} %encode.1), channel_id=1, replica_groups=mesh['layer'=8,'facet'=32] {'facet'}, dimensions={0} | all-to-all | bytes 2097152 | tf_op jit(solution)/shard_map/all_to_all | solution.py:235
  54.6 0.0 copy-start.1
  54.6 0.0 copy-start.8
  54.6 0.0 copy-done.3
  54.6 0.0 copy-done.4
  54.6 0.0 copy-done.5
  54.7 0.0 copy-done.6
  54.7 2.7 %subgrid.1 = bf16[8,16,512]{2,1,0:T(8,128)(2,1)S(1)} custom-call(bf16[32,128,128]{2,1,0:T(8,128)(2,1)S(1)} %all_to_all.15.recv_ref, bf16[128,512]{1,0:T(8,128)(2,1)S(1)} %copy-done.3, f32[32,512]{1,0:T(8,128)S(1)} %copy-done.5, f32[32,512]{1,0:T(8,128)S(1)} %copy-done.4, s32[64,512]{1,0:T(8,128)S(1)} %bitcast.4), custom_call_target="tpu_custom_call" | custom-call | tf_op jit(solution)/shard_map/subgrid/pallas_call | solution.py:237
  57.4 11.2 %all_to_all.16.recv_ref = bf16[8,16,512]{2,1,0:T(8,128)(2,1)S(1)} all-to-all(bf16[8,16,512]{2,1,0:T(8,128)(2,1)S(1)} %subgrid.1), channel_id=1, replica_groups=mesh['layer'=8,'facet'=32] {'layer'}, dimensions={0} | all-to-all | bytes 262144 | tf_op jit(solution)/shard_map/all_to_all | solution.py:247
  68.5 0.3 back.1
  68.9 16.1 %all_to_all.17.recv_ref = bf16[32,16,128]{2,1,0:T(8,128)(2,1)S(1)} all-to-all(bf16[32,16,128]{2,1,0:T(8,128)(2,1)S(1)} %back.1), channel_id=1, replica_groups=mesh['layer'=8,'facet'=32] {'facet'}, dimensions={0} | all-to-all | bytes 262144 | tf_op jit(solution)/shard_map/all_to_all | solution.py:259
  84.9 0.0 copy-done.1
  84.9 0.0 copy-done.8
  84.9 2.0 %decode.1 = f32[2,8,3072]{2,1,0:T(8,128)} custom-call(bf16[32,16,128]{2,1,0:T(8,128)(2,1)S(1)} %all_to_all.17.recv_ref, f32[1,3072]{1,0:T(1,128)S(1)} %bitcast.6, f32[32,24]{1,0:T(8,128)S(1)} %get-tuple-element.8.hc_ref, f32[32,24]{1,0:T(8,128)S(1)} %get-tuple-element.7.hs_ref, f32[32,128]{1,0:T(8,128)S(1)} %get-tuple-element.6.lc_ref, ...), custom_call_target="tpu_custom_call" | custom-call | tf_op jit(solution)/shard_map/decode/pallas_call | solution.py:261
  (2 shorter events, 0.0 us)
Async XLA Ops:
  1.0 1.4 %copy-start = (bf16[256,3072]{1,0:T(8,128)(2,1)S(1)}, bf16[256,3072]{1,0:T(8,128)(2,1)}, u32[]{:S(2)}) copy-start(bf16[256,3072]{1,0:T(8,128)(2,1)} %constant.98.clone.table_ref) | copy-start | bytes 4718596
  2.4 1.1 %copy-start.2 = (bf16[1,2,64,3072]{3,2,1,0:T(8,128)(2,1)S(1)}, bf16[1,2,64,3072]{3,2,1,0:T(8,128)(2,1)}, u32[]{:S(2)}) copy-start(bf16[1,2,64,3072]{3,2,1,0:T(8,128)(2,1)} %param.8) | copy-start | bytes 2359300
  3.6 0.7 copy-start.7
  14.0 40.7 %copy-start.3 = (bf16[128,512]{1,0:T(8,128)(2,1)S(1)}, bf16[128,512]{1,0:T(8,128)(2,1)}, u32[]{:S(2)}) copy-start(bf16[128,512]{1,0:T(8,128)(2,1)} %constant.99.clone.kernel_ref) | copy-start | bytes 393220
  14.0 40.7 %copy-start.4 = (f32[32,512]{1,0:T(8,128)S(1)}, f32[32,512]{1,0:T(8,128)}, u32[]{:S(2)}) copy-start(f32[32,512]{1,0:T(8,128)} %constant.101.clone.sin_ref) | copy-start | bytes 196612
  14.0 40.6 %copy-start.5 = (f32[32,512]{1,0:T(8,128)S(1)}, f32[32,512]{1,0:T(8,128)}, u32[]{:S(2)}) copy-start(f32[32,512]{1,0:T(8,128)} %constant.100.clone.cos_ref) | copy-start | bytes 196612
  14.0 40.6 %copy-start.6 = (s32[1,64,512]{2,1,0:T(8,128)S(1)}, s32[1,64,512]{2,1,0:T(8,128)}, u32[]{:S(2)}) copy-start(s32[1,64,512]{2,1,0:T(8,128)} %param.10) | copy-start | bytes 393220
  54.6 30.3 %copy-start.1 = (bf16[256,3072]{1,0:T(8,128)(2,1)S(1)}, bf16[256,3072]{1,0:T(8,128)(2,1)}, u32[]{:S(2)}) copy-start(bf16[256,3072]{1,0:T(8,128)(2,1)} %constant.98.clone.table_ref) | copy-start | bytes 4718596
  54.6 30.3 %copy-start.8 = (f32[3072]{0:T(1024)S(1)}, f32[3072]{0:T(1024)}, u32[]{:S(2)}) copy-start(f32[3072]{0:T(1024)} %param.9) | copy-start | bytes 36868

commit v2 on v1

--- a/solution.py
+++ b/solution.py
@@ -12,23 +12,11 @@
 CONTRIB = 128
 SUB = 512
 LANES = 128
-GROUP = 4
+GROUP = 8
 
 two_pi = 2.0 * math.pi
 NT = (((1,), (1,)), ((), ()))
 NN = (((1,), (0,)), ((), ()))
-
-
-def mulmod(left_term, right_term, modulus):
-    upper_part = right_term // 256
-    lower_part = right_term % 256
-    return jnp.mod(jnp.mod(left_term * upper_part, modulus) * 256 + left_term * lower_part, modulus)
-
-
-def offset_phases(offsets, places, image_width):
-    phase_turns = mulmod(offsets[:, None], places[None, :], image_width)
-    phase_angle = phase_turns.astype(jnp.float32) * (two_pi / image_width)
-    return jnp.cos(phase_angle), jnp.sin(phase_angle)
 
 
 def step_table(facet_width, image_width, sample_step):
@@ -52,18 +40,35 @@
     return np.cos(angle).astype(np.float32), np.sin(angle).astype(np.float32)
 
 
-def fill_phases(hc_ref, hs_ref, lc_ref, ls_ref, pr_ref, pi_ref):
-    lc, ls = lc_ref[...], ls_ref[...]
-    for tile in range(pr_ref.shape[1] // LANES):
-        hc = hc_ref[:, tile : tile + 1]
-        hs = hs_ref[:, tile : tile + 1]
+def offset_tables(offsets_ref, position, tiles, image_width):
+    subgrids = offsets_ref.shape[1]
+    down = lax.broadcasted_iota(jnp.int32, (subgrids, subgrids), 0)
+    across = lax.broadcasted_iota(jnp.int32, (subgrids, subgrids), 1)
+    column = jnp.sum(jnp.where(down == across, offsets_ref[...], 0), axis=1, keepdims=True)
+    lane = lax.broadcasted_iota(jnp.int32, (subgrids, LANES), 1)
+
+    def parts(product, modulus):
+        whole = jnp.floor(product.astype(jnp.float32) * (1.0 / modulus)).astype(jnp.int32)
+        angle = (product - whole * modulus).astype(jnp.float32) * (two_pi / modulus)
+        return jnp.cos(angle), jnp.sin(angle)
+
+    high = parts(column * (position * tiles + lane), image_width // LANES)
+    low = parts(column * lane, image_width)
+    return high + low
+
+
+def phases(tables, width):
+    hc, hs, lc, ls = tables
+    for tile in range(width // LANES):
+        c = hc[:, tile : tile + 1]
+        s = hs[:, tile : tile + 1]
         span = slice(tile * LANES, (tile + 1) * LANES)
-        pr_ref[:, span] = hc * lc - hs * ls
-        pi_ref[:, span] = hs * lc + hc * ls
+        yield span, c * lc - s * ls, s * lc + c * ls
 
 
 def encode_kernel(
-    slab_ref, window_ref, hc_ref, hs_ref, lc_ref, ls_ref, table_ref, out_ref, w_ref, pr_ref, pi_ref
+    slab_hbm, window_hbm, offsets_ref, table_hbm, out_ref, tables_ref,
+    slab_ref, window_ref, table_ref, w_ref, p_ref, sems,
 ):
     columns = slab_ref.shape[0] // 2
     width = slab_ref.shape[1]
@@ -71,25 +76,46 @@
 
     @pl.when(step == 0)
     def _():
-        fill_phases(hc_ref, hs_ref, lc_ref, ls_ref, pr_ref, pi_ref)
+        copies = [
+            pltpu.make_async_copy(slab_hbm, slab_ref, sems.at[0]),
+            pltpu.make_async_copy(window_hbm, window_ref, sems.at[1]),
+            pltpu.make_async_copy(table_hbm, table_ref, sems.at[2]),
+        ]
+        for copy in copies:
+            copy.start()
+        tables = offset_tables(
+            offsets_ref, lax.axis_index("facet"), width // LANES, width * offsets_ref.shape[1]
+        )
+        for k in range(4):
+            tables_ref[k] = tables[k]
+        for span, pr, pi in phases(tables, width):
+            p_ref[0, :, span] = pr
+            p_ref[1, :, span] = pr - pi
+            p_ref[2, :, span] = pr + pi
+        copies[0].wait()
+        copies[1].wait()
         for tile in range(width // 256):
             span = slice(tile * 256, (tile + 1) * 256)
             windowed = slab_ref[:, span].astype(jnp.float32) * window_ref[:, span]
-            w_ref[:, span] = windowed.astype(jnp.bfloat16).astype(jnp.float32)
+            windowed = windowed.astype(jnp.bfloat16).astype(jnp.float32)
+            w_ref[0 : 2 * columns, span] = windowed
+            w_ref[2 * columns :, span] = windowed[:columns] + windowed[columns:]
+        copies[2].wait()
 
     total = None
     for tile in range(width // 256):
         span = slice(tile * 256, (tile + 1) * 256)
         wr = w_ref[0:columns, span]
         wi = w_ref[columns : 2 * columns, span]
+        both = w_ref[2 * columns :, span]
         rows = []
         for k in range(GROUP):
-            pr = pr_ref[pl.ds(step * GROUP + k, 1), span]
-            pi = pi_ref[pl.ds(step * GROUP + k, 1), span]
-            rows.append((pr * wr + pi * wi).astype(jnp.bfloat16))
-            rows.append((pr * wi - pi * wr).astype(jnp.bfloat16))
+            real, less, more = (p_ref[n, pl.ds(step * GROUP + k, 1), span] for n in range(3))
+            shared = real * both
+            rows.append((shared - less * wi).astype(jnp.bfloat16))
+            rows.append((shared - more * wr).astype(jnp.bfloat16))
         part = lax.dot_general(
-            jnp.concatenate(rows, 0), table_ref[:, span], NT, preferred_element_type=jnp.float32
+            jnp.concatenate(rows, 0), table_ref[span, :], NN, preferred_element_type=jnp.float32
         )
         total = part if total is None else total + part
     scale = width ** (-0.5)
@@ -162,12 +188,14 @@
 
 
 def decode_kernel(
-    recv_ref, window_ref, hc_ref, hs_ref, lc_ref, ls_ref, table_ref, out_ref, pr_ref, pi_ref
+    recv_ref, window_ref, tables_ref, table_ref, out_ref, pr_ref, pi_ref
 ):
     subgrids = recv_ref.shape[0]
     per = recv_ref.shape[1] // 2
     width = out_ref.shape[2]
-    fill_phases(hc_ref, hs_ref, lc_ref, ls_ref, pr_ref, pi_ref)
+    for span, pr, pi in phases([tables_ref[k] for k in range(4)], width):
+        pr_ref[:, span] = pr
+        pi_ref[:, span] = pi
     rows = recv_ref[...].astype(jnp.float32)
     re, im = rows[:, :per], rows[:, per:]
     left_re = jnp.concatenate([re, im], 2).reshape(subgrids * per, 2 * CONTRIB).astype(jnp.bfloat16)
@@ -193,44 +221,49 @@
         out_ref[1, :, span] = out_im * taper
 
 
-def params(**more):
-    return pltpu.CompilerParams(vmem_limit_bytes=48 * 2**20, **more)
+def params(mebibytes):
+    return pltpu.CompilerParams(vmem_limit_bytes=mebibytes * 2**20)
 
 
 def shards(slabs, window, density, offsets):
     layers = lax.axis_size("layer")
     facets = lax.axis_size("facet")
-    position = lax.axis_index("facet")
     columns, width = slabs.shape[2], slabs.shape[3]
     per = columns // layers
     sample_step = SUB // CONTRIB
     image_width = width * facets
-    tiles = width // LANES
-    table = jnp.asarray(step_table(width, image_width, sample_step))
+    steps = step_table(width, image_width, sample_step)
+    table, table_down = jnp.asarray(steps), jnp.asarray(np.ascontiguousarray(steps.T))
     spread = jnp.asarray(kernel_table(sample_step))
     cos_u, sin_u = (jnp.asarray(part) for part in centre_phases(facets))
 
-    residues = jnp.mod(offsets, image_width)
-    starts = position * width + LANES * jnp.arange(tiles, dtype=jnp.int32)
-    hc, hs = offset_phases(residues, starts, image_width)
-    lc, ls = offset_phases(residues, jnp.arange(LANES, dtype=jnp.int32), image_width)
     window_row = window.reshape(1, width)
 
     whole = pl.BlockSpec(memory_space=pltpu.VMEM)
-    outgoing = pl.pallas_call(
+    anywhere = pl.BlockSpec(memory_space=pl.ANY)
+    outgoing, tables = pl.pallas_call(
         encode_kernel,
         grid=(facets // GROUP,),
-        out_shape=jax.ShapeDtypeStruct((facets, 2 * columns, CONTRIB), jnp.bfloat16),
-        in_specs=[whole] * 7,
-        out_specs=pl.BlockSpec((GROUP, 2 * columns, CONTRIB), lambda g: (g, 0, 0)),
+        out_shape=(
+            jax.ShapeDtypeStruct((facets, 2 * columns, CONTRIB), jnp.bfloat16),
+            jax.ShapeDtypeStruct((4, facets, LANES), jnp.float32),
+        ),
+        in_specs=[anywhere, anywhere, whole, anywhere],
+        out_specs=(
+            pl.BlockSpec((GROUP, 2 * columns, CONTRIB), lambda g: (g, 0, 0)),
+            pl.BlockSpec((4, facets, LANES), lambda g: (0, 0, 0)),
+        ),
         scratch_shapes=[
-            pltpu.VMEM((2 * columns, width), jnp.float32),
-            pltpu.VMEM((facets, width), jnp.float32),
-            pltpu.VMEM((facets, width), jnp.float32),
+            pltpu.VMEM((2 * columns, width), jnp.bfloat16),
+            pltpu.VMEM((1, width), jnp.float32),
+            pltpu.VMEM((width, 2 * CONTRIB), jnp.bfloat16),
+            pltpu.VMEM((3 * columns, width), jnp.float32),
+            pltpu.VMEM((3, facets, width), jnp.float32),
+            pltpu.SemaphoreType.DMA((3,)),
         ],
-        compiler_params=params(),
+        compiler_params=params(60),
         name="encode",
-    )(slabs.reshape(2 * columns, width), window_row, hc, hs, lc, ls, table)
+    )(slabs.reshape(2 * columns, width), window_row, offsets.reshape(1, facets), table_down)
 
     received = lax.all_to_all(outgoing, "facet", split_axis=0, concat_axis=0, tiled=True)
 
@@ -240,7 +273,7 @@
         in_specs=[whole] * 5,
         out_specs=whole,
         scratch_shapes=[pltpu.VMEM((columns, SUB), jnp.float32)] * 2,
-        compiler_params=params(),
+        compiler_params=params(48),
         name="subgrid",
     )(received, spread, cos_u, sin_u, density[0])
 
@@ -252,7 +285,7 @@
         in_specs=[whole] * 4,
         out_specs=whole,
         scratch_shapes=[pltpu.VMEM((facets * 2 * per, SUB), jnp.bfloat16)],
-        compiler_params=params(),
+        compiler_params=params(48),
         name="back",
     )(by_layer, spread, cos_u, sin_u)
 
@@ -261,12 +294,12 @@
     return pl.pallas_call(
         decode_kernel,
         out_shape=jax.ShapeDtypeStruct((2, per, width), jnp.float32),
-        in_specs=[whole] * 7,
+        in_specs=[whole] * 4,
         out_specs=whole,
         scratch_shapes=[pltpu.VMEM((facets, width), jnp.float32)] * 2,
-        compiler_params=params(),
+        compiler_params=params(48),
         name="decode",
-    )(returned, window_row, hc, hs, lc, ls, table)
+    )(returned, window_row, tables, table)
 
 
 def solution(mesh):

time: 87.3 us -> 84.4 us (0.967)
  local copies, waits for them, and re-layouts: 3.28 us -> 0.04 us
  Pallas kernels: 14.7 us -> 15.8 us
  other arithmetic: 1.02 us -> 0 us
    unnamed x18 -> x14, local copies, waits for them, and re-layouts: 3.28 us -> 0.04 us
    pallas_call x1, Pallas kernels: 9.68 us -> 10.9 us  [shards(): pl.pallas_call(encode_kernel, grid=(facets // GROUP,), out_shape=(jax.Sha...]
    all_to_all x1, blocking collectives: 40.6 us -> 41.6 us  [shards(): lax.all_to_all(outgoing, 'facet', split_axis=0, concat_axis=0, tiled=True)]
where the time goes in v2:
time: 84.4 us; the launch traced here: 84.1 us
  blocking collectives  68.1 us (81%)
  Pallas kernels  15.8 us (19%)
    all_to_all x1, blocking collectives, shards(): lax.all_to_all(outgoing, 'facet', split_axis=0, concat_axis=0, tiled=True)  41.6 us
    all_to_all x1, blocking collectives, shards(): lax.all_to_all(back_out, 'facet', split_axis=0, concat_axis=0, tiled=True)  16.1 us
    pallas_call x1, Pallas kernels, shards(): pl.pallas_call(encode_kernel, grid=(facets // GROUP,), out_shape=(jax.Sha...  10.9 us
    all_to_all x1, blocking collectives, shards(): lax.all_to_all(gridded, 'layer', split_axis=0, concat_axis=0, tiled=True)  10.4 us
    pallas_call x1, Pallas kernels, shards(): pl.pallas_call(grid_kernel, out_shape=jax.ShapeDtypeStruct((layers, 2 * p...  2.69 us
    pallas_call x1, Pallas kernels, shards(): pl.pallas_call(decode_kernel, out_shape=jax.ShapeDtypeStruct((2, per, wid...  1.94 us

profile of v2, /device:TPU:1, one launch (start us, length us, event | category | flops | bytes accessed | tf_op | source)
XLA Modules:
  0.0 84.1 jit_solution(7061971783522170658)
XLA Ops:
  0.0 10.9 %encode.1 = (bf16[32,128,128]{2,1,0:T(8,128)(2,1)}, f32[4,32,128]{2,1,0:T(8,128)}) custom-call(bf16[128,3072]{1,0:T(8,128)(2,1)} %bitcast.7, f32[1,3072]{1,0:T(1,128)} %bitcast.5, s32[1,32]{1,0:T(1,128)} %bitcast.8, bf16[3072,256]{1,0:T(8,128)(2,1)} %constant.11.clone.table_hbm), custom_call_target="tpu_custom_call" | custom-call | tf_op jit(solution)/shard_map/encode/pallas_call | solution.py:244
  10.9 0.0 copy-start.1
  10.9 0.0 copy-start.2
  11.0 0.0 copy-start.3
  11.0 0.0 copy-start.4
  11.0 41.6 %all_to_all.15.recv_ref = bf16[32,128,128]{2,1,0:T(8,128)(2,1)S(1)} all-to-all(bf16[32,128,128]{2,1,0:T(8,128)(2,1)} %get-tuple-element.7), channel_id=1, replica_groups=mesh['layer'=8,'facet'=32] {'facet'}, dimensions={0} | all-to-all | bytes 2097152 | tf_op jit(solution)/shard_map/all_to_all | solution.py:268
  52.6 0.0 copy-start
  52.6 0.0 copy-start.5
  52.6 0.0 copy-start.6
  52.6 0.0 copy-done.1
  52.6 0.0 copy-done.2
  52.6 0.0 copy-done.3
  52.6 0.0 copy-done.4
  52.6 2.7 %subgrid.1 = bf16[8,16,512]{2,1,0:T(8,128)(2,1)S(1)} custom-call(bf16[32,128,128]{2,1,0:T(8,128)(2,1)S(1)} %all_to_all.15.recv_ref, bf16[128,512]{1,0:T(8,128)(2,1)S(1)} %copy-done.1, f32[32,512]{1,0:T(8,128)S(1)} %copy-done.3, f32[32,512]{1,0:T(8,128)S(1)} %copy-done.2, s32[64,512]{1,0:T(8,128)S(1)} %bitcast.4), custom_call_target="tpu_custom_call" | custom-call | tf_op jit(solution)/shard_map/subgrid/pallas_call | solution.py:270
  55.3 10.4 %all_to_all.16.recv_ref = bf16[8,16,512]{2,1,0:T(8,128)(2,1)S(1)} all-to-all(bf16[8,16,512]{2,1,0:T(8,128)(2,1)S(1)} %subgrid.1), channel_id=1, replica_groups=mesh['layer'=8,'facet'=32] {'layer'}, dimensions={0} | all-to-all | bytes 262144 | tf_op jit(solution)/shard_map/all_to_all | solution.py:280
  65.7 0.3 back.1
  66.0 16.1 %all_to_all.17.recv_ref = bf16[32,16,128]{2,1,0:T(8,128)(2,1)S(1)} all-to-all(bf16[32,16,128]{2,1,0:T(8,128)(2,1)S(1)} %back.1), channel_id=1, replica_groups=mesh['layer'=8,'facet'=32] {'facet'}, dimensions={0} | all-to-all | bytes 262144 | tf_op jit(solution)/shard_map/all_to_all | solution.py:292
  82.1 0.0 copy-done
  82.1 0.0 copy-done.5
  82.1 0.0 copy-done.6
  82.1 1.9 %decode.1 = f32[2,8,3072]{2,1,0:T(8,128)} custom-call(bf16[32,16,128]{2,1,0:T(8,128)(2,1)S(1)} %all_to_all.17.recv_ref, f32[1,3072]{1,0:T(1,128)S(1)} %bitcast.6, f32[4,32,128]{2,1,0:T(8,128)S(1)} %copy-done.5, bf16[256,3072]{1,0:T(8,128)(2,1)S(1)} %copy-done), custom_call_target="tpu_custom_call" | custom-call | tf_op jit(solution)/shard_map/decode/pallas_call | solution.py:294
Async XLA Ops:
  10.9 41.7 %copy-start.1 = (bf16[128,512]{1,0:T(8,128)(2,1)S(1)}, bf16[128,512]{1,0:T(8,128)(2,1)}, u32[]{:S(2)}) copy-start(bf16[128,512]{1,0:T(8,128)(2,1)} %constant.12.clone.kernel_ref) | copy-start | bytes 393220
  10.9 41.7 %copy-start.2 = (f32[32,512]{1,0:T(8,128)S(1)}, f32[32,512]{1,0:T(8,128)}, u32[]{:S(2)}) copy-start(f32[32,512]{1,0:T(8,128)} %constant.14.clone.sin_ref) | copy-start | bytes 196612
  11.0 41.7 %copy-start.3 = (f32[32,512]{1,0:T(8,128)S(1)}, f32[32,512]{1,0:T(8,128)}, u32[]{:S(2)}) copy-start(f32[32,512]{1,0:T(8,128)} %constant.13.clone.cos_ref) | copy-start | bytes 196612
  11.0 41.7 %copy-start.4 = (s32[1,64,512]{2,1,0:T(8,128)S(1)}, s32[1,64,512]{2,1,0:T(8,128)}, u32[]{:S(2)}) copy-start(s32[1,64,512]{2,1,0:T(8,128)} %param.11) | copy-start | bytes 393220
  52.6 29.5 %copy-start = (bf16[256,3072]{1,0:T(8,128)(2,1)S(1)}, bf16[256,3072]{1,0:T(8,128)(2,1)}, u32[]{:S(2)}) copy-start(bf16[256,3072]{1,0:T(8,128)(2,1)} %constant.10.clone.table_ref) | copy-start | bytes 4718596
  52.6 29.5 %copy-start.5 = (f32[4,32,128]{2,1,0:T(8,128)S(1)}, f32[4,32,128]{2,1,0:T(8,128)}, u32[]{:S(2)}) copy-start(f32[4,32,128]{2,1,0:T(8,128)} %get-tuple-element.8.tables_ref) | copy-start | bytes 196612
  52.6 29.5 %copy-start.6 = (f32[3072]{0:T(1024)S(1)}, f32[3072]{0:T(1024)}, u32[]{:S(2)}) copy-start(f32[3072]{0:T(1024)} %param.10) | copy-start | bytes 36868

commit v3 on v2

--- a/solution.py
+++ b/solution.py
@@ -12,7 +12,8 @@
 CONTRIB = 128
 SUB = 512
 LANES = 128
-GROUP = 8
+FINE = 4
+STEP = 256
 
 two_pi = 2.0 * math.pi
 NT = (((1,), (1,)), ((), ()))
@@ -26,6 +27,24 @@
     return np.concatenate([np.cos(angle), np.sin(angle)], 0).astype(ml_dtypes.bfloat16)
 
 
+def fold_tables(facet_width, image_width, sample_step):
+    k = np.arange(facet_width // 2, dtype=np.int64)[None, :]
+    j1 = np.arange(CONTRIB // FINE, dtype=np.int64)[:, None]
+    j2 = np.arange(FINE, dtype=np.int64)[:, None]
+
+    def parts(turns):
+        angle = np.mod(turns, image_width) * (2.0 * np.pi / image_width)
+        return np.stack([np.cos(angle), np.sin(angle)]).astype(np.float32)
+
+    half_step = sample_step * FINE // 2
+    coarse = parts(half_step * j1 * (2 * k + 1))
+    fine = np.stack([parts(sample_step * j2 * k), parts(-sample_step * j2 * (k + 1))])
+    fine = fine.transpose(2, 0, 1, 3).reshape(4 * FINE, facet_width // 2)
+    turn = np.broadcast_to(parts(half_step * j1), (2, CONTRIB // FINE, LANES))
+    flip = np.eye(STEP)[::-1].astype(ml_dtypes.bfloat16)
+    return coarse, np.ascontiguousarray(fine), np.ascontiguousarray(turn), np.ascontiguousarray(flip)
+
+
 def kernel_table(sample_step):
     spacing = np.arange(SUB)[None, :] - sample_step * np.arange(CONTRIB)[:, None]
     scaled = spacing / sample_step
@@ -40,8 +59,9 @@
     return np.cos(angle).astype(np.float32), np.sin(angle).astype(np.float32)
 
 
-def offset_tables(offsets_ref, position, tiles, image_width):
+def offset_tables(offsets_ref, position, width):
     subgrids = offsets_ref.shape[1]
+    image_width = width * subgrids
     down = lax.broadcasted_iota(jnp.int32, (subgrids, subgrids), 0)
     across = lax.broadcasted_iota(jnp.int32, (subgrids, subgrids), 1)
     column = jnp.sum(jnp.where(down == across, offsets_ref[...], 0), axis=1, keepdims=True)
@@ -52,83 +72,101 @@
         angle = (product - whole * modulus).astype(jnp.float32) * (two_pi / modulus)
         return jnp.cos(angle), jnp.sin(angle)
 
-    high = parts(column * (position * tiles + lane), image_width // LANES)
-    low = parts(column * lane, image_width)
-    return high + low
-
-
-def phases(tables, width):
-    hc, hs, lc, ls = tables
-    for tile in range(width // LANES):
-        c = hc[:, tile : tile + 1]
-        s = hs[:, tile : tile + 1]
-        span = slice(tile * LANES, (tile + 1) * LANES)
-        yield span, c * lc - s * ls, s * lc + c * ls
+    facet_turns = jnp.bitwise_and(column * position, subgrids - 1)
+    return {
+        "start": parts(column * (position * (width // LANES) + lane), image_width // LANES),
+        "cell": parts(column * lane, image_width),
+        "tile": parts(column * lane, image_width // LANES),
+        "inner": parts(column * (2 * lane + 1), 2 * image_width),
+        "middle": parts(
+            column * (width - 1) + 2 * width * facet_turns + 0 * lane, 2 * image_width
+        ),
+    }
 
 
 def encode_kernel(
-    slab_hbm, window_hbm, offsets_ref, table_hbm, out_ref, tables_ref,
-    slab_ref, window_ref, table_ref, w_ref, p_ref, sems,
+    slab_hbm, window_hbm, offsets_ref, coarse_hbm, fine_hbm, turn_hbm, flip_hbm, out_ref, tables_ref,
+    slab_ref, window_ref, coarse_ref, fine_ref, turn_ref, flip_ref,
+    phase_ref, cos_ref, sin_ref, even_ref, odd_ref, total_ref, sems,
 ):
     columns = slab_ref.shape[0] // 2
     width = slab_ref.shape[1]
-    step = pl.program_id(0)
-
-    @pl.when(step == 0)
-    def _():
-        copies = [
-            pltpu.make_async_copy(slab_hbm, slab_ref, sems.at[0]),
-            pltpu.make_async_copy(window_hbm, window_ref, sems.at[1]),
-            pltpu.make_async_copy(table_hbm, table_ref, sems.at[2]),
-        ]
-        for copy in copies:
-            copy.start()
-        tables = offset_tables(
-            offsets_ref, lax.axis_index("facet"), width // LANES, width * offsets_ref.shape[1]
+    half = width // 2
+    subgrids = offsets_ref.shape[1]
+    rows = CONTRIB // FINE
+    pairs = (
+        (slab_hbm, slab_ref), (window_hbm, window_ref), (coarse_hbm, coarse_ref),
+        (fine_hbm, fine_ref), (turn_hbm, turn_ref), (flip_hbm, flip_ref),
+    )
+    copies = [pltpu.make_async_copy(a, b, sems.at[n]) for n, (a, b) in enumerate(pairs)]
+    for copy in copies:
+        copy.start()
+    turns = offset_tables(offsets_ref, lax.axis_index("facet"), width)
+    for n in range(2):
+        tables_ref[n] = turns["start"][n]
+        tables_ref[2 + n] = turns["cell"][n]
+    high, low, centre = turns["tile"], turns["inner"], turns["middle"]
+    for tile in range(half // LANES):
+        c, s = high[0][:, tile : tile + 1], high[1][:, tile : tile + 1]
+        span = slice(tile * LANES, (tile + 1) * LANES)
+        phase_ref[0, :, span] = c * low[0] - s * low[1]
+        phase_ref[1, :, span] = s * low[0] + c * low[1]
+    for copy in copies:
+        copy.wait()
+
+    def windowed(span):
+        product = slab_ref[:, span].astype(jnp.float32) * window_ref[:, span]
+        return product.astype(jnp.bfloat16)
+
+    for tile in range(half // STEP):
+        span = slice(tile * STEP, (tile + 1) * STEP)
+        plus = windowed(slice(half + tile * STEP, half + (tile + 1) * STEP)).astype(jnp.float32)
+        minus = lax.dot_general(
+            windowed(slice(half - (tile + 1) * STEP, half - tile * STEP)), flip_ref[...], NN,
+            preferred_element_type=jnp.float32,
         )
-        for k in range(4):
-            tables_ref[k] = tables[k]
-        for span, pr, pi in phases(tables, width):
-            p_ref[0, :, span] = pr
-            p_ref[1, :, span] = pr - pi
-            p_ref[2, :, span] = pr + pi
-        copies[0].wait()
-        copies[1].wait()
-        for tile in range(width // 256):
-            span = slice(tile * 256, (tile + 1) * 256)
-            windowed = slab_ref[:, span].astype(jnp.float32) * window_ref[:, span]
-            windowed = windowed.astype(jnp.bfloat16).astype(jnp.float32)
-            w_ref[0 : 2 * columns, span] = windowed
-            w_ref[2 * columns :, span] = windowed[:columns] + windowed[columns:]
-        copies[2].wait()
-
-    total = None
-    for tile in range(width // 256):
-        span = slice(tile * 256, (tile + 1) * 256)
-        wr = w_ref[0:columns, span]
-        wi = w_ref[columns : 2 * columns, span]
-        both = w_ref[2 * columns :, span]
-        rows = []
-        for k in range(GROUP):
-            real, less, more = (p_ref[n, pl.ds(step * GROUP + k, 1), span] for n in range(3))
-            shared = real * both
-            rows.append((shared - less * wi).astype(jnp.bfloat16))
-            rows.append((shared - more * wr).astype(jnp.bfloat16))
+        for fine in range(FINE):
+            sides = []
+            for n, side in enumerate((plus, minus)):
+                re, im = side[:columns], side[columns:]
+                if fine > 0:
+                    row = (2 * fine + n) * 2
+                    c, s = fine_ref[row : row + 1, span], fine_ref[row + 1 : row + 2, span]
+                    re, im = re * c + im * s, im * c - re * s
+                sides.append((re, im))
+            (re_p, im_p), (re_m, im_m) = sides
+            base = 2 * columns * fine
+            even_ref[base : base + columns] = (re_p + re_m).astype(jnp.bfloat16)
+            even_ref[base + columns : base + 2 * columns] = (im_p + im_m).astype(jnp.bfloat16)
+            odd_ref[base : base + columns] = (im_p - im_m).astype(jnp.bfloat16)
+            odd_ref[base + columns : base + 2 * columns] = (re_m - re_p).astype(jnp.bfloat16)
+        cj, sj = coarse_ref[0, :, span], coarse_ref[1, :, span]
+        for s in range(subgrids):
+            co, so = phase_ref[0, s : s + 1, span], phase_ref[1, s : s + 1, span]
+            cos_ref[s * rows : (s + 1) * rows] = (co * cj - so * sj).astype(jnp.bfloat16)
+            sin_ref[s * rows : (s + 1) * rows] = (so * cj + co * sj).astype(jnp.bfloat16)
         part = lax.dot_general(
-            jnp.concatenate(rows, 0), table_ref[span, :], NN, preferred_element_type=jnp.float32
-        )
-        total = part if total is None else total + part
+            cos_ref[...], even_ref[...], NT, preferred_element_type=jnp.float32
+        ) + lax.dot_general(sin_ref[...], odd_ref[...], NT, preferred_element_type=jnp.float32)
+        if tile == 0:
+            total_ref[...] = part
+        else:
+            total_ref[...] += part
+
+    cj, sj = turn_ref[0], turn_ref[1]
     scale = width ** (-0.5)
-    for k in range(GROUP):
-        base = 2 * columns * k
-        upper = total[base : base + columns]
-        lower = total[base + columns : base + 2 * columns]
-        out_ref[k, 0:columns, :] = (
-            (upper[:, :CONTRIB] - lower[:, CONTRIB:]) * scale
-        ).astype(jnp.bfloat16)
-        out_ref[k, columns : 2 * columns, :] = (
-            (upper[:, CONTRIB:] + lower[:, :CONTRIB]) * scale
-        ).astype(jnp.bfloat16)
+    sign = jnp.where(
+        lax.broadcasted_iota(jnp.int32, (1, 2 * columns), 1) < columns, scale, -scale
+    )
+    for s in range(subgrids):
+        co, so = centre[0][s : s + 1], centre[1][s : s + 1]
+        c = (co * cj + so * sj) * scale
+        d = (so * cj - co * sj) * sign
+        blocks = []
+        for fine in range(FINE):
+            block = total_ref[s * rows : (s + 1) * rows, fine * LANES : (fine + 1) * LANES]
+            blocks.append(block * c + pltpu.roll(block, columns, 1) * d)
+        out_ref[s] = jnp.concatenate(blocks, 0).T.astype(jnp.bfloat16)
 
 
 def grid_kernel(recv_ref, kernel_ref, cos_ref, sin_ref, counts_ref, out_ref, re_ref, im_ref):
@@ -193,9 +231,11 @@
     subgrids = recv_ref.shape[0]
     per = recv_ref.shape[1] // 2
     width = out_ref.shape[2]
-    for span, pr, pi in phases([tables_ref[k] for k in range(4)], width):
-        pr_ref[:, span] = pr
-        pi_ref[:, span] = pi
+    for tile in range(width // LANES):
+        c, s = tables_ref[0, :, tile : tile + 1], tables_ref[1, :, tile : tile + 1]
+        span = slice(tile * LANES, (tile + 1) * LANES)
+        pr_ref[:, span] = c * tables_ref[2] - s * tables_ref[3]
+        pi_ref[:, span] = s * tables_ref[2] + c * tables_ref[3]
     rows = recv_ref[...].astype(jnp.float32)
     re, im = rows[:, :per], rows[:, per:]
     left_re = jnp.concatenate([re, im], 2).reshape(subgrids * per, 2 * CONTRIB).astype(jnp.bfloat16)
@@ -232,38 +272,47 @@
     per = columns // layers
     sample_step = SUB // CONTRIB
     image_width = width * facets
-    steps = step_table(width, image_width, sample_step)
-    table, table_down = jnp.asarray(steps), jnp.asarray(np.ascontiguousarray(steps.T))
-    spread = jnp.asarray(kernel_table(sample_step))
+    table = jnp.asarray(step_table(width, image_width, sample_step))
+    folds = [jnp.asarray(part) for part in fold_tables(width, image_width, sample_step)]
+    spreading = kernel_table(sample_step)
+    spread = jnp.asarray(spreading)
+    order = np.arange(CONTRIB).reshape(CONTRIB // FINE, FINE).T.reshape(-1)
+    spread_in = jnp.asarray(np.ascontiguousarray(spreading[order]))
     cos_u, sin_u = (jnp.asarray(part) for part in centre_phases(facets))
 
     window_row = window.reshape(1, width)
 
     whole = pl.BlockSpec(memory_space=pltpu.VMEM)
     anywhere = pl.BlockSpec(memory_space=pl.ANY)
+    rows = facets * CONTRIB // FINE
+    wide = 2 * columns * FINE
+    half = width // 2
     outgoing, tables = pl.pallas_call(
         encode_kernel,
-        grid=(facets // GROUP,),
         out_shape=(
             jax.ShapeDtypeStruct((facets, 2 * columns, CONTRIB), jnp.bfloat16),
             jax.ShapeDtypeStruct((4, facets, LANES), jnp.float32),
         ),
-        in_specs=[anywhere, anywhere, whole, anywhere],
-        out_specs=(
-            pl.BlockSpec((GROUP, 2 * columns, CONTRIB), lambda g: (g, 0, 0)),
-            pl.BlockSpec((4, facets, LANES), lambda g: (0, 0, 0)),
-        ),
+        in_specs=[anywhere, anywhere, whole] + [anywhere] * 4,
+        out_specs=(whole, whole),
         scratch_shapes=[
             pltpu.VMEM((2 * columns, width), jnp.bfloat16),
             pltpu.VMEM((1, width), jnp.float32),
-            pltpu.VMEM((width, 2 * CONTRIB), jnp.bfloat16),
-            pltpu.VMEM((3 * columns, width), jnp.float32),
-            pltpu.VMEM((3, facets, width), jnp.float32),
-            pltpu.SemaphoreType.DMA((3,)),
+            pltpu.VMEM((2, CONTRIB // FINE, half), jnp.float32),
+            pltpu.VMEM((4 * FINE, half), jnp.float32),
+            pltpu.VMEM((2, CONTRIB // FINE, LANES), jnp.float32),
+            pltpu.VMEM((STEP, STEP), jnp.bfloat16),
+            pltpu.VMEM((2, facets, half), jnp.float32),
+            pltpu.VMEM((rows, STEP), jnp.bfloat16),
+            pltpu.VMEM((rows, STEP), jnp.bfloat16),
+            pltpu.VMEM((wide, STEP), jnp.bfloat16),
+            pltpu.VMEM((wide, STEP), jnp.bfloat16),
+            pltpu.VMEM((rows, wide), jnp.float32),
+            pltpu.SemaphoreType.DMA((6,)),
         ],
         compiler_params=params(60),
         name="encode",
-    )(slabs.reshape(2 * columns, width), window_row, offsets.reshape(1, facets), table_down)
+    )(slabs.reshape(2 * columns, width), window_row, offsets.reshape(1, facets), *folds)
 
     received = lax.all_to_all(outgoing, "facet", split_axis=0, concat_axis=0, tiled=True)
 
@@ -275,7 +324,7 @@
         scratch_shapes=[pltpu.VMEM((columns, SUB), jnp.float32)] * 2,
         compiler_params=params(48),
         name="subgrid",
-    )(received, spread, cos_u, sin_u, density[0])
+    )(received, spread_in, cos_u, sin_u, density[0])
 
     by_layer = lax.all_to_all(gridded, "layer", split_axis=0, concat_axis=0, tiled=True)
 

time: 84.4 us -> 82.6 us (0.979)
  Pallas kernels: 15.8 us -> 14.1 us
    pallas_call x1, Pallas kernels: 10.9 us -> 9.12 us  [shards(): pl.pallas_call(encode_kernel, out_shape=(jax.ShapeDtypeStruct((facets, 2...]
    all_to_all x1, blocking collectives: 10.4 us -> 11.2 us  [shards(): lax.all_to_all(gridded, 'layer', split_axis=0, concat_axis=0, tiled=True)]
where the time goes in v3:
time: 82.6 us; the launch traced here: 82.3 us
  blocking collectives  68.1 us (82%)
  Pallas kernels  14.1 us (17%)
    all_to_all x1, blocking collectives, shards(): lax.all_to_all(outgoing, 'facet', split_axis=0, concat_axis=0, tiled=True)  40.8 us
    all_to_all x1, blocking collectives, shards(): lax.all_to_all(back_out, 'facet', split_axis=0, concat_axis=0, tiled=True)  16 us
    all_to_all x1, blocking collectives, shards(): lax.all_to_all(gridded, 'layer', split_axis=0, concat_axis=0, tiled=True)  11.2 us
    pallas_call x1, Pallas kernels, shards(): pl.pallas_call(encode_kernel, out_shape=(jax.ShapeDtypeStruct((facets, 2...  9.12 us
    pallas_call x1, Pallas kernels, shards(): pl.pallas_call(grid_kernel, out_shape=jax.ShapeDtypeStruct((layers, 2 * p...  2.69 us
    pallas_call x1, Pallas kernels, shards(): pl.pallas_call(decode_kernel, out_shape=jax.ShapeDtypeStruct((2, per, wid...  1.97 us

profile of v3, /device:TPU:1, one launch (start us, length us, event | category | flops | bytes accessed | tf_op | source)
XLA Modules:
  0.0 82.3 jit_solution(5759416715457098248)
XLA Ops:
  0.0 0.0 copy-start.1
  0.0 0.0 copy-start.2
  0.0 0.0 copy-start.3
  0.0 0.0 copy-start.4
  0.0 9.1 %encode.1 = (bf16[32,128,128]{2,1,0:T(8,128)(2,1)}, f32[4,32,128]{2,1,0:T(8,128)}) custom-call(bf16[128,3072]{1,0:T(8,128)(2,1)} %bitcast.7, f32[1,3072]{1,0:T(1,128)} %bitcast.5, s32[1,32]{1,0:T(1,128)} %bitcast.8, f32[2,32,1536]{2,1,0:T(8,128)} %constant.19.clone.coarse_hbm, f32[16,1536]{1,0:T(8,128)} %constant.20.clone.fine_hbm, ...), custom_call_target="tpu_custom_call" | custom-call | tf_op jit(solution)/shard_map/encode/pallas_call | solution.py:290
  9.1 0.0 copy-start.5
  9.2 40.8 %all_to_all.15.recv_ref = bf16[32,128,128]{2,1,0:T(8,128)(2,1)S(1)} all-to-all(bf16[32,128,128]{2,1,0:T(8,128)(2,1)} %get-tuple-element.7), channel_id=1, replica_groups=mesh['layer'=8,'facet'=32] {'facet'}, dimensions={0} | all-to-all | bytes 2097152 | tf_op jit(solution)/shard_map/all_to_all | solution.py:317
  50.0 0.0 copy-start
  50.0 0.0 copy-start.6
  50.0 0.0 copy-start.7
  50.0 0.0 copy-done.1
  50.0 0.0 copy-done.2
  50.0 0.0 copy-done.3
  50.0 0.0 copy-done.4
  50.0 2.7 %subgrid.1 = bf16[8,16,512]{2,1,0:T(8,128)(2,1)S(1)} custom-call(bf16[32,128,128]{2,1,0:T(8,128)(2,1)S(1)} %all_to_all.15.recv_ref, bf16[128,512]{1,0:T(8,128)(2,1)S(1)} %copy-done.4, f32[32,512]{1,0:T(8,128)S(1)} %copy-done.2, f32[32,512]{1,0:T(8,128)S(1)} %copy-done.1, s32[64,512]{1,0:T(8,128)S(1)} %bitcast.4), custom_call_target="tpu_custom_call" | custom-call | tf_op jit(solution)/shard_map/subgrid/pallas_call | solution.py:319
  52.7 11.2 %all_to_all.16.recv_ref = bf16[8,16,512]{2,1,0:T(8,128)(2,1)S(1)} all-to-all(bf16[8,16,512]{2,1,0:T(8,128)(2,1)S(1)} %subgrid.1), channel_id=1, replica_groups=mesh['layer'=8,'facet'=32] {'layer'}, dimensions={0} | all-to-all | bytes 262144 | tf_op jit(solution)/shard_map/all_to_all | solution.py:329
  64.0 0.0 copy-done.5
  64.0 0.3 back.1
  64.3 16.0 %all_to_all.17.recv_ref = bf16[32,16,128]{2,1,0:T(8,128)(2,1)S(1)} all-to-all(bf16[32,16,128]{2,1,0:T(8,128)(2,1)S(1)} %back.1), channel_id=1, replica_groups=mesh['layer'=8,'facet'=32] {'facet'}, dimensions={0} | all-to-all | bytes 262144 | tf_op jit(solution)/shard_map/all_to_all | solution.py:341
  80.3 0.0 copy-done
  80.3 0.0 copy-done.6
  80.3 0.0 copy-done.7
  80.3 2.0 %decode.1 = f32[2,8,3072]{2,1,0:T(8,128)} custom-call(bf16[32,16,128]{2,1,0:T(8,128)(2,1)S(1)} %all_to_all.17.recv_ref, f32[1,3072]{1,0:T(1,128)S(1)} %bitcast.6, f32[4,32,128]{2,1,0:T(8,128)S(1)} %copy-done.6, bf16[256,3072]{1,0:T(8,128)(2,1)S(1)} %copy-done), custom_call_target="tpu_custom_call" | custom-call | tf_op jit(solution)/shard_map/decode/pallas_call | solution.py:343
Async XLA Ops:
  0.0 50.0 %copy-start.1 = (f32[32,512]{1,0:T(8,128)S(1)}, f32[32,512]{1,0:T(8,128)}, u32[]{:S(2)}) copy-start(f32[32,512]{1,0:T(8,128)} %constant.26.clone.sin_ref) | copy-start | bytes 196612
  0.0 50.0 %copy-start.2 = (f32[32,512]{1,0:T(8,128)S(1)}, f32[32,512]{1,0:T(8,128)}, u32[]{:S(2)}) copy-start(f32[32,512]{1,0:T(8,128)} %constant.25.clone.cos_ref) | copy-start | bytes 196612
  0.0 50.0 %copy-start.3 = (s32[1,64,512]{2,1,0:T(8,128)S(1)}, s32[1,64,512]{2,1,0:T(8,128)}, u32[]{:S(2)}) copy-start(s32[1,64,512]{2,1,0:T(8,128)} %param.15) | copy-start | bytes 393220
  0.0 50.0 %copy-start.4 = (bf16[128,512]{1,0:T(8,128)(2,1)S(1)}, bf16[128,512]{1,0:T(8,128)(2,1)}, u32[]{:S(2)}) copy-start(bf16[128,512]{1,0:T(8,128)(2,1)} %constant.24.clone.kernel_ref) | copy-start | bytes 393220
  9.1 54.8 %copy-start.5 = (bf16[128,512]{1,0:T(8,128)(2,1)S(1)}, bf16[128,512]{1,0:T(8,128)(2,1)}, u32[]{:S(2)}) copy-start(bf16[128,512]{1,0:T(8,128)(2,1)} %constant.23.clone.kernel_ref) | copy-start | bytes 393220
  50.0 30.3 %copy-start = (bf16[256,3072]{1,0:T(8,128)(2,1)S(1)}, bf16[256,3072]{1,0:T(8,128)(2,1)}, u32[]{:S(2)}) copy-start(bf16[256,3072]{1,0:T(8,128)(2,1)} %constant.18.clone.table_ref) | copy-start | bytes 4718596
  50.0 30.3 %copy-start.6 = (f32[4,32,128]{2,1,0:T(8,128)S(1)}, f32[4,32,128]{2,1,0:T(8,128)}, u32[]{:S(2)}) copy-start(f32[4,32,128]{2,1,0:T(8,128)} %get-tuple-element.8.tables_ref) | copy-start | bytes 196612
  50.0 30.3 %copy-start.7 = (f32[3072]{0:T(1024)S(1)}, f32[3072]{0:T(1024)}, u32[]{:S(2)}) copy-start(f32[3072]{0:T(1024)} %param.14) | copy-start | bytes 36868

commit v4 on v3

--- a/solution.py
+++ b/solution.py
@@ -14,6 +14,7 @@
 LANES = 128
 FINE = 4
 STEP = 256
+BLOCKS = 2
 
 two_pi = 2.0 * math.pi
 NT = (((1,), (1,)), ((), ()))
@@ -87,7 +88,7 @@
 def encode_kernel(
     slab_hbm, window_hbm, offsets_ref, coarse_hbm, fine_hbm, turn_hbm, flip_hbm, out_ref, tables_ref,
     slab_ref, window_ref, coarse_ref, fine_ref, turn_ref, flip_ref,
-    phase_ref, cos_ref, sin_ref, even_ref, odd_ref, total_ref, sems,
+    phase_ref, side_ref, turn_table_ref, wave_ref, total_ref, sems,
 ):
     columns = slab_ref.shape[0] // 2
     width = slab_ref.shape[1]
@@ -118,86 +119,119 @@
         product = slab_ref[:, span].astype(jnp.float32) * window_ref[:, span]
         return product.astype(jnp.bfloat16)
 
-    for tile in range(half // STEP):
+    def stage_columns(tile, fine):
         span = slice(tile * STEP, (tile + 1) * STEP)
-        plus = windowed(slice(half + tile * STEP, half + (tile + 1) * STEP)).astype(jnp.float32)
-        minus = lax.dot_general(
-            windowed(slice(half - (tile + 1) * STEP, half - tile * STEP)), flip_ref[...], NN,
-            preferred_element_type=jnp.float32,
-        )
-        for fine in range(FINE):
-            sides = []
-            for n, side in enumerate((plus, minus)):
-                re, im = side[:columns], side[columns:]
-                if fine > 0:
-                    row = (2 * fine + n) * 2
-                    c, s = fine_ref[row : row + 1, span], fine_ref[row + 1 : row + 2, span]
-                    re, im = re * c + im * s, im * c - re * s
-                sides.append((re, im))
-            (re_p, im_p), (re_m, im_m) = sides
-            base = 2 * columns * fine
-            even_ref[base : base + columns] = (re_p + re_m).astype(jnp.bfloat16)
-            even_ref[base + columns : base + 2 * columns] = (im_p + im_m).astype(jnp.bfloat16)
-            odd_ref[base : base + columns] = (im_p - im_m).astype(jnp.bfloat16)
-            odd_ref[base + columns : base + 2 * columns] = (re_m - re_p).astype(jnp.bfloat16)
+        slot = tile % 2
+        if fine == 0:
+            side_ref[0] = windowed(
+                slice(half + tile * STEP, half + (tile + 1) * STEP)
+            ).astype(jnp.float32)
+            side_ref[1] = lax.dot_general(
+                windowed(slice(half - (tile + 1) * STEP, half - tile * STEP)), flip_ref[...], NN,
+                preferred_element_type=jnp.float32,
+            )
+        sides = []
+        for n in range(2):
+            re, im = side_ref[n, :columns], side_ref[n, columns:]
+            if fine > 0:
+                row = (2 * fine + n) * 2
+                c, s = fine_ref[row : row + 1, span], fine_ref[row + 1 : row + 2, span]
+                re, im = re * c + im * s, im * c - re * s
+            sides.append((re, im))
+        (re_p, im_p), (re_m, im_m) = sides
+        upper = slice(2 * columns * fine, 2 * columns * fine + columns)
+        lower = slice(2 * columns * fine + columns, 2 * columns * (fine + 1))
+        wave_ref[slot, upper, :STEP] = (re_p + re_m).astype(jnp.bfloat16)
+        wave_ref[slot, lower, :STEP] = (im_p + im_m).astype(jnp.bfloat16)
+        wave_ref[slot, upper, STEP:] = (im_p - im_m).astype(jnp.bfloat16)
+        wave_ref[slot, lower, STEP:] = (re_m - re_p).astype(jnp.bfloat16)
+
+    def stage_rows(tile, s):
+        span = slice(tile * STEP, (tile + 1) * STEP)
+        where = slice(s * rows, (s + 1) * rows)
         cj, sj = coarse_ref[0, :, span], coarse_ref[1, :, span]
-        for s in range(subgrids):
-            co, so = phase_ref[0, s : s + 1, span], phase_ref[1, s : s + 1, span]
-            cos_ref[s * rows : (s + 1) * rows] = (co * cj - so * sj).astype(jnp.bfloat16)
-            sin_ref[s * rows : (s + 1) * rows] = (so * cj + co * sj).astype(jnp.bfloat16)
-        part = lax.dot_general(
-            cos_ref[...], even_ref[...], NT, preferred_element_type=jnp.float32
-        ) + lax.dot_general(sin_ref[...], odd_ref[...], NT, preferred_element_type=jnp.float32)
-        if tile == 0:
-            total_ref[...] = part
-        else:
-            total_ref[...] += part
-
-    cj, sj = turn_ref[0], turn_ref[1]
+        co, so = phase_ref[0, s : s + 1, span], phase_ref[1, s : s + 1, span]
+        turn_table_ref[tile % 2, where, :STEP] = (co * cj - so * sj).astype(jnp.bfloat16)
+        turn_table_ref[tile % 2, where, STEP:] = (so * cj + co * sj).astype(jnp.bfloat16)
+
+    cm, sm = turn_ref[0], turn_ref[1]
     scale = width ** (-0.5)
     sign = jnp.where(
         lax.broadcasted_iota(jnp.int32, (1, 2 * columns), 1) < columns, scale, -scale
     )
-    for s in range(subgrids):
+
+    def finish(s):
         co, so = centre[0][s : s + 1], centre[1][s : s + 1]
-        c = (co * cj + so * sj) * scale
-        d = (so * cj - co * sj) * sign
+        c = (co * cm + so * sm) * scale
+        d = (so * cm - co * sm) * sign
         blocks = []
         for fine in range(FINE):
             block = total_ref[s * rows : (s + 1) * rows, fine * LANES : (fine + 1) * LANES]
             blocks.append(block * c + pltpu.roll(block, columns, 1) * d)
         out_ref[s] = jnp.concatenate(blocks, 0).T.astype(jnp.bfloat16)
 
-
-def grid_kernel(recv_ref, kernel_ref, cos_ref, sin_ref, counts_ref, out_ref, re_ref, im_ref):
+    steps = half // STEP
+    each = subgrids // BLOCKS
+    for fine in range(FINE):
+        stage_columns(0, fine)
+    for s in range(subgrids):
+        stage_rows(0, s)
+    for tile in range(steps):
+        for block in range(BLOCKS):
+            where = slice(block * each * rows, (block + 1) * each * rows)
+            part = lax.dot_general(
+                turn_table_ref[tile % 2, where], wave_ref[tile % 2], NT,
+                preferred_element_type=jnp.float32,
+            )
+            if tile == 0:
+                total_ref[where] = part
+            else:
+                total_ref[where] += part
+            if tile + 1 < steps:
+                for fine in range(block * FINE // BLOCKS, (block + 1) * FINE // BLOCKS):
+                    stage_columns(tile + 1, fine)
+                for s in range(block * each, (block + 1) * each):
+                    stage_rows(tile + 1, s)
+            else:
+                for s in range(block * each, (block + 1) * each):
+                    finish(s)
+
+
+def grid_kernel(
+    recv_ref, kernel_ref, cos_ref, sin_ref, counts_ref, part_ref, out_ref, re_ref, im_ref
+):
     facets = recv_ref.shape[0]
     columns = recv_ref.shape[1] // 2
+    cells = re_ref.shape[1]
+    half = facets // 2
     re_ref[...] = jnp.zeros_like(re_ref)
     im_ref[...] = jnp.zeros_like(im_ref)
 
-    def body(block, carry):
-        re, im = None, None
-        for k in range(4):
-            f = block * 4 + k
-            spread = lax.dot_general(
-                recv_ref[f], kernel_ref[...], NN, preferred_element_type=jnp.float32
+    for f in range(facets // 4):
+        first, second, third, fourth = (
+            recv_ref[n].astype(jnp.float32) for n in (f, f + half, facets - 1 - f, half - 1 - f)
+        )
+        for parity in range(2):
+            span = slice(parity * cells // 2, (parity + 1) * cells // 2)
+            near = first + second if parity == 0 else first - second
+            far = third + fourth if parity == 0 else third - fourth
+            both = jnp.concatenate([near + far, near - far], 0).astype(jnp.bfloat16)
+            wide = lax.dot_general(
+                both, kernel_ref[:, span], NN, preferred_element_type=jnp.float32
             )
-            c = cos_ref[pl.ds(f, 1), :]
-            s = sin_ref[pl.ds(f, 1), :]
-            a, b = spread[:columns], spread[columns:]
-            re_term = a * c + b * s
-            im_term = b * c - a * s
-            re = re_term if re is None else re + re_term
-            im = im_term if im is None else im + im_term
-        re_ref[...] += re
-        im_ref[...] += im
-        return carry
-
-    lax.fori_loop(0, facets // 4, body, 0)
-    counts = counts_ref[...]
-    weights = jnp.where(
-        counts > 0, 1.0 / jnp.maximum(counts, 1).astype(jnp.float32), 0.0
-    ) * ((2 * facets) ** (-0.5))
+            even_re, even_im = wide[:columns], wide[columns : 2 * columns]
+            odd_re, odd_im = wide[2 * columns : 3 * columns], wide[3 * columns :]
+            c, s = cos_ref[f : f + 1, span], sin_ref[f : f + 1, span]
+            re_ref[:, span] += even_re * c + odd_im * s
+            im_ref[:, span] += even_im * c - odd_re * s
+
+    counts = lax.dot_general(
+        counts_ref[...].astype(jnp.float32).astype(jnp.bfloat16), part_ref[...], NN,
+        preferred_element_type=jnp.float32,
+    )
+    weights = jnp.where(counts > 0, 1.0 / jnp.maximum(counts, 1.0), 0.0) * (
+        (2 * facets) ** (-0.5)
+    )
     re = re_ref[...] * weights
     im = im_ref[...] * weights
     per = out_ref.shape[1] // 2
@@ -274,11 +308,15 @@
     image_width = width * facets
     table = jnp.asarray(step_table(width, image_width, sample_step))
     folds = [jnp.asarray(part) for part in fold_tables(width, image_width, sample_step)]
-    spreading = kernel_table(sample_step)
+    cells = np.concatenate([np.arange(0, SUB, 2), np.arange(1, SUB, 2)])
+    spreading = np.ascontiguousarray(kernel_table(sample_step)[:, cells])
+    parting = np.eye(SUB)[:, cells].astype(ml_dtypes.bfloat16)
     spread = jnp.asarray(spreading)
     order = np.arange(CONTRIB).reshape(CONTRIB // FINE, FINE).T.reshape(-1)
     spread_in = jnp.asarray(np.ascontiguousarray(spreading[order]))
-    cos_u, sin_u = (jnp.asarray(part) for part in centre_phases(facets))
+    cos_u, sin_u = (
+        jnp.asarray(np.ascontiguousarray(part[:, cells])) for part in centre_phases(facets)
+    )
 
     window_row = window.reshape(1, width)
 
@@ -303,10 +341,9 @@
             pltpu.VMEM((2, CONTRIB // FINE, LANES), jnp.float32),
             pltpu.VMEM((STEP, STEP), jnp.bfloat16),
             pltpu.VMEM((2, facets, half), jnp.float32),
-            pltpu.VMEM((rows, STEP), jnp.bfloat16),
-            pltpu.VMEM((rows, STEP), jnp.bfloat16),
-            pltpu.VMEM((wide, STEP), jnp.bfloat16),
-            pltpu.VMEM((wide, STEP), jnp.bfloat16),
+            pltpu.VMEM((2, 2 * columns, STEP), jnp.float32),
+            pltpu.VMEM((2, rows, 2 * STEP), jnp.bfloat16),
+            pltpu.VMEM((2, wide, 2 * STEP), jnp.bfloat16),
             pltpu.VMEM((rows, wide), jnp.float32),
             pltpu.SemaphoreType.DMA((6,)),
         ],
@@ -319,12 +356,12 @@
     gridded = pl.pallas_call(
         grid_kernel,
         out_shape=jax.ShapeDtypeStruct((layers, 2 * per, SUB), jnp.bfloat16),
-        in_specs=[whole] * 5,
+        in_specs=[whole] * 6,
         out_specs=whole,
         scratch_shapes=[pltpu.VMEM((columns, SUB), jnp.float32)] * 2,
         compiler_params=params(48),
         name="subgrid",
-    )(received, spread_in, cos_u, sin_u, density[0])
+    )(received, spread_in, cos_u, sin_u, density[0], jnp.asarray(parting))
 
     by_layer = lax.all_to_all(gridded, "layer", split_axis=0, concat_axis=0, tiled=True)
 

time: 82.6 us -> 79.9 us (0.967)
  Pallas kernels: 14.1 us -> 11.5 us
    pallas_call x1, Pallas kernels: 2.69 us -> 0.87 us  [shards(): pl.pallas_call(grid_kernel, out_shape=jax.ShapeDtypeStruct((layers, 2 * p...]
where the time goes in v4:
time: 79.9 us; the launch traced here: 79.6 us
  blocking collectives  68 us (85%)
  Pallas kernels  11.5 us (14%)
    all_to_all x1, blocking collectives, shards(): lax.all_to_all(outgoing, 'facet', split_axis=0, concat_axis=0, tiled=True)  40.7 us
    all_to_all x1, blocking collectives, shards(): lax.all_to_all(back_out, 'facet', split_axis=0, concat_axis=0, tiled=True)  16.1 us
    all_to_all x1, blocking collectives, shards(): lax.all_to_all(gridded, 'layer', split_axis=0, concat_axis=0, tiled=True)  11.2 us
    pallas_call x1, Pallas kernels, shards(): pl.pallas_call(encode_kernel, out_shape=(jax.ShapeDtypeStruct((facets, 2...  8.35 us
    pallas_call x1, Pallas kernels, shards(): pl.pallas_call(decode_kernel, out_shape=jax.ShapeDtypeStruct((2, per, wid...  1.98 us

profile of v4, /device:TPU:1, one launch (start us, length us, event | category | flops | bytes accessed | tf_op | source)
XLA Modules:
  0.0 79.6 jit_solution(13762562930712081428)
XLA Ops:
  0.0 0.0 copy-start.1
  0.0 0.0 copy-start.2
  0.0 0.0 copy-start.3
  0.0 0.0 copy-start.4
  0.0 0.0 copy-start.5
  0.0 8.3 %encode.1 = (bf16[32,128,128]{2,1,0:T(8,128)(2,1)}, f32[4,32,128]{2,1,0:T(8,128)}) custom-call(bf16[128,3072]{1,0:T(8,128)(2,1)} %bitcast.7, f32[1,3072]{1,0:T(1,128)} %bitcast.5, s32[1,32]{1,0:T(1,128)} %bitcast.8, f32[2,32,1536]{2,1,0:T(8,128)} %constant.21.clone.coarse_hbm, f32[16,1536]{1,0:T(8,128)} %constant.22.clone.fine_hbm, ...), custom_call_target="tpu_custom_call" | custom-call | tf_op jit(solution)/shard_map/encode/pallas_call | solution.py:328
  8.4 40.7 %all_to_all.15.recv_ref = bf16[32,128,128]{2,1,0:T(8,128)(2,1)S(1)} all-to-all(bf16[32,128,128]{2,1,0:T(8,128)(2,1)} %get-tuple-element.7), channel_id=1, replica_groups=mesh['layer'=8,'facet'=32] {'facet'}, dimensions={0} | all-to-all | bytes 2097152 | tf_op jit(solution)/shard_map/all_to_all | solution.py:354
  49.1 0.0 copy-start.6
  49.1 0.0 copy-done.1
  49.1 0.0 copy-done.2
  49.1 0.0 copy-done.3
  49.1 0.0 copy-done.4
  49.1 0.0 copy-done.5
  49.1 0.0 copy-start
  49.1 0.0 copy-start.7
  49.1 0.0 copy-start.8
  49.1 0.9 %subgrid.1 = bf16[8,16,512]{2,1,0:T(8,128)(2,1)S(1)} custom-call(bf16[32,128,128]{2,1,0:T(8,128)(2,1)S(1)} %all_to_all.15.recv_ref, bf16[128,512]{1,0:T(8,128)(2,1)S(1)} %copy-done.5, f32[32,512]{1,0:T(8,128)S(1)} %copy-done.3, f32[32,512]{1,0:T(8,128)S(1)} %copy-done.2, s32[64,512]{1,0:T(8,128)S(1)} %bitcast.4, bf16[512,512]{1,0:T(8,128)(2,1)S(1)} %copy-done.1), custom_call_target="tpu_custom_call" | custom-call | tf_op jit(solution)/shard_map/subgrid/pallas_call | solution.py:356
  50.0 11.2 %all_to_all.16.recv_ref = bf16[8,16,512]{2,1,0:T(8,128)(2,1)S(1)} all-to-all(bf16[8,16,512]{2,1,0:T(8,128)(2,1)S(1)} %subgrid.1), channel_id=1, replica_groups=mesh['layer'=8,'facet'=32] {'layer'}, dimensions={0} | all-to-all | bytes 262144 | tf_op jit(solution)/shard_map/all_to_all | solution.py:366
  61.2 0.0 copy-done.6
  61.2 0.3 back.1
  61.5 16.1 %all_to_all.17.recv_ref = bf16[32,16,128]{2,1,0:T(8,128)(2,1)S(1)} all-to-all(bf16[32,16,128]{2,1,0:T(8,128)(2,1)S(1)} %back.1), channel_id=1, replica_groups=mesh['layer'=8,'facet'=32] {'facet'}, dimensions={0} | all-to-all | bytes 262144 | tf_op jit(solution)/shard_map/all_to_all | solution.py:378
  77.6 0.0 copy-done
  77.6 0.0 copy-done.7
  77.6 0.0 copy-done.8
  77.6 2.0 %decode.1 = f32[2,8,3072]{2,1,0:T(8,128)} custom-call(bf16[32,16,128]{2,1,0:T(8,128)(2,1)S(1)} %all_to_all.17.recv_ref, f32[1,3072]{1,0:T(1,128)S(1)} %bitcast.6, f32[4,32,128]{2,1,0:T(8,128)S(1)} %copy-done.7, bf16[256,3072]{1,0:T(8,128)(2,1)S(1)} %copy-done), custom_call_target="tpu_custom_call" | custom-call | tf_op jit(solution)/shard_map/decode/pallas_call | solution.py:380
Async XLA Ops:
  0.0 49.1 %copy-start.1 = (bf16[512,512]{1,0:T(8,128)(2,1)S(1)}, bf16[512,512]{1,0:T(8,128)(2,1)}, u32[]{:S(2)}) copy-start(bf16[512,512]{1,0:T(8,128)(2,1)} %constant.29.clone.part_ref) | copy-start | bytes 1572868
  0.0 49.1 %copy-start.2 = (f32[32,512]{1,0:T(8,128)S(1)}, f32[32,512]{1,0:T(8,128)}, u32[]{:S(2)}) copy-start(f32[32,512]{1,0:T(8,128)} %constant.28.clone.sin_ref) | copy-start | bytes 196612
  0.0 49.1 %copy-start.3 = (f32[32,512]{1,0:T(8,128)S(1)}, f32[32,512]{1,0:T(8,128)}, u32[]{:S(2)}) copy-start(f32[32,512]{1,0:T(8,128)} %constant.27.clone.cos_ref) | copy-start | bytes 196612
  0.0 49.1 %copy-start.4 = (s32[1,64,512]{2,1,0:T(8,128)S(1)}, s32[1,64,512]{2,1,0:T(8,128)}, u32[]{:S(2)}) copy-start(s32[1,64,512]{2,1,0:T(8,128)} %param.16) | copy-start | bytes 393220
  0.0 49.1 %copy-start.5 = (bf16[128,512]{1,0:T(8,128)(2,1)S(1)}, bf16[128,512]{1,0:T(8,128)(2,1)}, u32[]{:S(2)}) copy-start(bf16[128,512]{1,0:T(8,128)(2,1)} %constant.26.clone.kernel_ref) | copy-start | bytes 393220
  49.1 12.1 %copy-start.6 = (bf16[128,512]{1,0:T(8,128)(2,1)S(1)}, bf16[128,512]{1,0:T(8,128)(2,1)}, u32[]{:S(2)}) copy-start(bf16[128,512]{1,0:T(8,128)(2,1)} %constant.25.clone.kernel_ref) | copy-start | bytes 393220
  49.1 28.5 %copy-start = (bf16[256,3072]{1,0:T(8,128)(2,1)S(1)}, bf16[256,3072]{1,0:T(8,128)(2,1)}, u32[]{:S(2)}) copy-start(bf16[256,3072]{1,0:T(8,128)(2,1)} %constant.20.clone.table_ref) | copy-start | bytes 4718596
  49.1 28.5 %copy-start.7 = (f32[4,32,128]{2,1,0:T(8,128)S(1)}, f32[4,32,128]{2,1,0:T(8,128)}, u32[]{:S(2)}) copy-start(f32[4,32,128]{2,1,0:T(8,128)} %get-tuple-element.8.tables_ref) | copy-start | bytes 196612
  49.1 28.5 %copy-start.8 = (f32[3072]{0:T(1024)S(1)}, f32[3072]{0:T(1024)}, u32[]{:S(2)}) copy-start(f32[3072]{0:T(1024)} %param.15) | copy-start | bytes 36868

commit v5 on v4

--- a/solution.py
+++ b/solution.py
@@ -168,7 +168,13 @@
         for fine in range(FINE):
             block = total_ref[s * rows : (s + 1) * rows, fine * LANES : (fine + 1) * LANES]
             blocks.append(block * c + pltpu.roll(block, columns, 1) * d)
-        out_ref[s] = jnp.concatenate(blocks, 0).T.astype(jnp.bfloat16)
+        down = jnp.concatenate(blocks, 0).T
+        per = out_ref.shape[2] // 2
+        for layer in range(out_ref.shape[0]):
+            first = layer * per
+            out_ref[layer, s] = jnp.concatenate(
+                [down[first : first + per], down[columns + first : columns + first + per]], 0
+            ).astype(jnp.bfloat16)
 
     steps = half // STEP
     each = subgrids // BLOCKS
@@ -197,64 +203,55 @@
                     finish(s)
 
 
-def grid_kernel(
-    recv_ref, kernel_ref, cos_ref, sin_ref, counts_ref, part_ref, out_ref, re_ref, im_ref
+def subgrid_kernel(
+    recv_ref, kernel_ref, cos_ref, sin_ref, counts_ref, part_ref, back_ref, out_ref,
+    re_ref, im_ref, rows_ref,
 ):
-    facets = recv_ref.shape[0]
-    columns = recv_ref.shape[1] // 2
+    layers, facets, tall, contrib = recv_ref.shape
+    per = tall // 2
     cells = re_ref.shape[1]
     half = facets // 2
-    re_ref[...] = jnp.zeros_like(re_ref)
-    im_ref[...] = jnp.zeros_like(im_ref)
-
     for f in range(facets // 4):
         first, second, third, fourth = (
-            recv_ref[n].astype(jnp.float32) for n in (f, f + half, facets - 1 - f, half - 1 - f)
+            recv_ref[:, n].astype(jnp.float32)
+            for n in (f, f + half, facets - 1 - f, half - 1 - f)
         )
         for parity in range(2):
             span = slice(parity * cells // 2, (parity + 1) * cells // 2)
             near = first + second if parity == 0 else first - second
             far = third + fourth if parity == 0 else third - fourth
-            both = jnp.concatenate([near + far, near - far], 0).astype(jnp.bfloat16)
+            both = jnp.concatenate([near + far, near - far], 0)
             wide = lax.dot_general(
-                both, kernel_ref[:, span], NN, preferred_element_type=jnp.float32
+                both.reshape(2 * layers * tall, contrib).astype(jnp.bfloat16),
+                kernel_ref[:, span], NN, preferred_element_type=jnp.float32,
+            ).reshape(2, layers, 2, per, cells // 2)
+            even_re, even_im, odd_re, odd_im = (
+                wide[a, :, b].reshape(layers * per, cells // 2) for a in range(2) for b in range(2)
             )
-            even_re, even_im = wide[:columns], wide[columns : 2 * columns]
-            odd_re, odd_im = wide[2 * columns : 3 * columns], wide[3 * columns :]
             c, s = cos_ref[f : f + 1, span], sin_ref[f : f + 1, span]
-            re_ref[:, span] += even_re * c + odd_im * s
-            im_ref[:, span] += even_im * c - odd_re * s
-
+            re = even_re * c + odd_im * s
+            im = even_im * c - odd_re * s
+            if f == 0:
+                re_ref[:, span] = re
+                im_ref[:, span] = im
+            else:
+                re_ref[:, span] += re
+                im_ref[:, span] += im
     counts = lax.dot_general(
-        counts_ref[...].astype(jnp.float32).astype(jnp.bfloat16), part_ref[...], NN,
-        preferred_element_type=jnp.float32,
+        counts_ref[...].reshape(layers * per, cells).astype(jnp.float32).astype(jnp.bfloat16),
+        part_ref[...], NN, preferred_element_type=jnp.float32,
     )
     weights = jnp.where(counts > 0, 1.0 / jnp.maximum(counts, 1.0), 0.0) * (
         (2 * facets) ** (-0.5)
     )
-    re = re_ref[...] * weights
-    im = im_ref[...] * weights
-    per = out_ref.shape[1] // 2
-    for layer in range(out_ref.shape[0]):
-        span = slice(layer * per, (layer + 1) * per)
-        out_ref[layer] = jnp.concatenate([re[span], im[span]], 0).astype(jnp.bfloat16)
-
-
-def back_kernel(recv_ref, kernel_ref, cos_ref, sin_ref, out_ref, rows_ref):
-    layers = recv_ref.shape[0]
-    facets = out_ref.shape[0]
-    total = recv_ref[0].astype(jnp.float32)
-    for layer in range(1, layers):
-        total = total + recv_ref[layer].astype(jnp.float32)
-    per = total.shape[0] // 2
-    re, im = total[:per], total[per:]
+    re = jnp.sum((re_ref[...] * weights).reshape(layers, per, cells), axis=0)
+    im = jnp.sum((im_ref[...] * weights).reshape(layers, per, cells), axis=0)
     for f in range(facets):
-        c = cos_ref[f : f + 1, :]
-        s = sin_ref[f : f + 1, :]
+        c, s = cos_ref[f : f + 1, :], sin_ref[f : f + 1, :]
         turned = jnp.concatenate([re * c - im * s, im * c + re * s], 0)
-        rows_ref[f * 2 * per : (f + 1) * 2 * per, :] = turned.astype(jnp.bfloat16)
+        rows_ref[f * tall : (f + 1) * tall, :] = turned.astype(jnp.bfloat16)
     back = lax.dot_general(
-        rows_ref[...], kernel_ref[...], NT, preferred_element_type=jnp.float32
+        rows_ref[...], back_ref[...], NT, preferred_element_type=jnp.float32
     )
     out_ref[...] = (back * 0.5).astype(jnp.bfloat16).reshape(out_ref.shape)
 
@@ -321,6 +318,9 @@
     window_row = window.reshape(1, width)
 
     whole = pl.BlockSpec(memory_space=pltpu.VMEM)
+    counts = lax.all_to_all(
+        density.reshape(layers, per, SUB), "layer", split_axis=0, concat_axis=0, tiled=True
+    )
     anywhere = pl.BlockSpec(memory_space=pl.ANY)
     rows = facets * CONTRIB // FINE
     wide = 2 * columns * FINE
@@ -328,7 +328,7 @@
     outgoing, tables = pl.pallas_call(
         encode_kernel,
         out_shape=(
-            jax.ShapeDtypeStruct((facets, 2 * columns, CONTRIB), jnp.bfloat16),
+            jax.ShapeDtypeStruct((layers, facets, 2 * per, CONTRIB), jnp.bfloat16),
             jax.ShapeDtypeStruct((4, facets, LANES), jnp.float32),
         ),
         in_specs=[anywhere, anywhere, whole] + [anywhere] * 4,
@@ -348,32 +348,31 @@
             pltpu.SemaphoreType.DMA((6,)),
         ],
         compiler_params=params(60),
+        cost_estimate=pl.CostEstimate(
+            flops=4 * rows * half * wide, bytes_accessed=4 * width * rows, transcendentals=0
+        ),
         name="encode",
     )(slabs.reshape(2 * columns, width), window_row, offsets.reshape(1, facets), *folds)
 
-    received = lax.all_to_all(outgoing, "facet", split_axis=0, concat_axis=0, tiled=True)
-
-    gridded = pl.pallas_call(
-        grid_kernel,
-        out_shape=jax.ShapeDtypeStruct((layers, 2 * per, SUB), jnp.bfloat16),
-        in_specs=[whole] * 6,
+    outgoing, counts = lax.optimization_barrier((outgoing, counts))
+    received = lax.all_to_all(
+        outgoing.reshape(layers * facets, 2 * per, CONTRIB), ("layer", "facet"),
+        split_axis=0, concat_axis=0, tiled=True,
+    ).reshape(layers, facets, 2 * per, CONTRIB)
+
+    back_out = pl.pallas_call(
+        subgrid_kernel,
+        out_shape=jax.ShapeDtypeStruct((facets, 2 * per, CONTRIB), jnp.bfloat16),
+        in_specs=[whole] * 7,
         out_specs=whole,
-        scratch_shapes=[pltpu.VMEM((columns, SUB), jnp.float32)] * 2,
+        scratch_shapes=[
+            pltpu.VMEM((columns, SUB), jnp.float32),
+            pltpu.VMEM((columns, SUB), jnp.float32),
+            pltpu.VMEM((facets * 2 * per, SUB), jnp.bfloat16),
+        ],
         compiler_params=params(48),
         name="subgrid",
-    )(received, spread_in, cos_u, sin_u, density[0], jnp.asarray(parting))
-
-    by_layer = lax.all_to_all(gridded, "layer", split_axis=0, concat_axis=0, tiled=True)
-
-    back_out = pl.pallas_call(
-        back_kernel,
-        out_shape=jax.ShapeDtypeStruct((facets, 2 * per, CONTRIB), jnp.bfloat16),
-        in_specs=[whole] * 4,
-        out_specs=whole,
-        scratch_shapes=[pltpu.VMEM((facets * 2 * per, SUB), jnp.bfloat16)],
-        compiler_params=params(48),
-        name="back",
-    )(by_layer, spread, cos_u, sin_u)
+    )(received, spread_in, cos_u, sin_u, counts, jnp.asarray(parting), spread)
 
     returned = lax.all_to_all(back_out, "facet", split_axis=0, concat_axis=0, tiled=True)
 

time: 79.9 us -> 79.2 us (level)
  blocking collectives: 68 us -> 60.9 us
  starting transfers between devices: 0 us -> 6.37 us
    all_to_all x0 -> x1, starting transfers between devices: none -> 6.37 us  [shards(): lax.all_to_all(density.reshape(layers, per, SUB), 'layer', split_axis=0,...]
    all_to_all x2 -> x1, blocking collectives: 51.9 us -> 46.6 us  [shards(): lax.all_to_all(outgoing.reshape(layers * facets, 2 * per, CONTRIB), ('lay...]
    all_to_all x1, blocking collectives: 16.1 us -> 14.3 us  [shards(): lax.all_to_all(back_out, 'facet', split_axis=0, concat_axis=0, tiled=True)]
    pallas_call x3 -> x2, Pallas kernels: 9.52 us -> 9.45 us  [the longest x1 8.28 us: shards(): pl.pallas_call(encode_kernel, out_shape=(jax.ShapeDtypeStruct((layers, fa...]
  transfers between devices with their start and end apart: 0 -> 1, of which waited for: 0 -> 0; matrix products, arithmetic and copies ran while one was open for 0% -> 0% of each run, Pallas kernels for 0% -> 10%
where the time goes in v5:
time: 79.2 us; the launch traced here: 78.9 us
  blocking collectives  60.9 us (77%)
  Pallas kernels  11.4 us (14%)
  starting transfers between devices  6.37 us (8%)
    all_to_all x1, blocking collectives, shards(): lax.all_to_all(outgoing.reshape(layers * facets, 2 * per, CONTRIB), ('lay...  46.6 us
    all_to_all x1, blocking collectives, shards(): lax.all_to_all(back_out, 'facet', split_axis=0, concat_axis=0, tiled=True)  14.3 us
    pallas_call x1, Pallas kernels, shards(): pl.pallas_call(encode_kernel, out_shape=(jax.ShapeDtypeStruct((layers, fa...  8.28 us
    all_to_all x1, starting transfers between devices, shards(): lax.all_to_all(density.reshape(layers, per, SUB), 'layer', split_axis=0,...  6.37 us
    pallas_call x1, Pallas kernels, shards(): pl.pallas_call(decode_kernel, out_shape=jax.ShapeDtypeStruct((2, per, wid...  1.98 us
  transfers between devices with their start and end apart: 1, of which 0 were waited for; matrix products, arithmetic and copies ran while one was open for 0% of the time, Pallas kernels for 10%

profile of v5, /device:TPU:1, one launch (start us, length us, event | category | flops | bytes accessed | tf_op | source)
XLA Modules:
  0.0 78.9 jit_solution(7487759493035507402)
XLA Ops:
  0.0 6.4 %all-to-all-start = ((s32[8,8,512]{2,1,0:T(8,128)}), s32[8,8,512]{2,1,0:T(8,128)S(1)}, u32[]{:S(2)}, u32[]{:S(2)}) async-start(s32[8,8,512]{2,1,0:T(8,128)} %bitcast.10), calls=%async_computation | async-start | bytes 262144 | tf_op jit(solution)/shard_map/all_to_all | solution.py:321
  6.4 8.3 %encode.1 = (bf16[8,32,16,128]{3,2,1,0:T(8,128)(2,1)}, f32[4,32,128]{2,1,0:T(8,128)}) custom-call(bf16[128,3072]{1,0:T(8,128)(2,1)} %bitcast.11, f32[1,3072]{1,0:T(1,128)} %bitcast.7, s32[1,32]{1,0:T(1,128)} %bitcast.12, f32[2,32,1536]{2,1,0:T(8,128)} %constant.21.clone.coarse_hbm, f32[16,1536]{1,0:T(8,128)} %constant.22.clone.fine_hbm, ...), custom_call_target="tpu_custom_call" | custom-call | flops 3221225472 | bytes 12582912 | tf_op jit(solution)/shard_map/encode/pallas_call | solution.py:328
  14.7 0.0 copy-start.1
  14.7 0.0 copy-start.2
  14.7 0.0 copy-start.3
  14.7 0.0 copy-start.4
  14.7 0.0 copy-start.5
  14.7 0.0 all-to-all-done.counts_ref
  14.7 46.6 %all_to_all.15 = bf16[256,16,128]{2,1,0:T(8,128)(2,1)S(1)} all-to-all(bf16[256,16,128]{2,1,0:T(8,128)(2,1)} %bitcast.9), channel_id=1, replica_groups=mesh['layer'=8,'facet'=32] {'layer','facet'}, dimensions={0} | all-to-all | bytes 2097152 | tf_op jit(solution)/shard_map/all_to_all | solution.py:358
  61.4 0.0 copy-start
  61.4 0.0 copy-start.6
  61.4 0.0 copy-start.7
  61.4 0.0 copy-done.1
  61.4 0.0 copy-done.2
  61.4 0.0 copy-done.3
  61.4 0.0 copy-done.4
  61.4 0.0 copy-done.5
  61.4 1.2 %subgrid.1 = bf16[32,16,128]{2,1,0:T(8,128)(2,1)S(1)} custom-call(bf16[8,32,16,128]{3,2,1,0:T(8,128)(2,1)S(1)} %bitcast.6, bf16[128,512]{1,0:T(8,128)(2,1)S(1)} %copy-done.2, f32[32,512]{1,0:T(8,128)S(1)} %copy-done.5, f32[32,512]{1,0:T(8,128)S(1)} %copy-done.4, s32[8,8,512]{2,1,0:T(8,128)S(1)} %all-to-all-done.counts_ref, bf16[512,512]{1,0:T(8,128)(2,1)S(1)} %copy-done.1, ...), custom_call_target="tpu_custom_call" | custom-call | tf_op jit(solution)/shard_map/subgrid/pallas_call | solution.py:363
  62.6 14.3 %all_to_all.16.recv_ref = bf16[32,16,128]{2,1,0:T(8,128)(2,1)S(1)} all-to-all(bf16[32,16,128]{2,1,0:T(8,128)(2,1)S(1)} %subgrid.1), channel_id=1, replica_groups=mesh['layer'=8,'facet'=32] {'facet'}, dimensions={0} | all-to-all | bytes 262144 | tf_op jit(solution)/shard_map/all_to_all | solution.py:377
  76.9 0.0 copy-done
  76.9 0.0 copy-done.6
  76.9 0.0 copy-done.7
  76.9 2.0 %decode.1 = f32[2,8,3072]{2,1,0:T(8,128)} custom-call(bf16[32,16,128]{2,1,0:T(8,128)(2,1)S(1)} %all_to_all.16.recv_ref, f32[1,3072]{1,0:T(1,128)S(1)} %bitcast.8, f32[4,32,128]{2,1,0:T(8,128)S(1)} %copy-done.6, bf16[256,3072]{1,0:T(8,128)(2,1)S(1)} %copy-done), custom_call_target="tpu_custom_call" | custom-call | tf_op jit(solution)/shard_map/decode/pallas_call | solution.py:379
Async XLA Ops:
  0.0 14.7 %all-to-all-start = ((s32[8,8,512]{2,1,0:T(8,128)}), s32[8,8,512]{2,1,0:T(8,128)S(1)}, u32[]{:S(2)}, u32[]{:S(2)}) async-start(s32[8,8,512]{2,1,0:T(8,128)} %bitcast.10), calls=%async_computation | async-start | bytes 262144 | tf_op jit(solution)/shard_map/all_to_all | solution.py:321
  14.7 46.7 %copy-start.1 = (bf16[512,512]{1,0:T(8,128)(2,1)S(1)}, bf16[512,512]{1,0:T(8,128)(2,1)}, u32[]{:S(2)}) copy-start(bf16[512,512]{1,0:T(8,128)(2,1)} %constant.29.clone.part_ref) | copy-start | bytes 1572868
  14.7 46.7 %copy-start.2 = (bf16[128,512]{1,0:T(8,128)(2,1)S(1)}, bf16[128,512]{1,0:T(8,128)(2,1)}, u32[]{:S(2)}) copy-start(bf16[128,512]{1,0:T(8,128)(2,1)} %constant.26.clone.kernel_ref) | copy-start | bytes 393220
  14.7 46.7 %copy-start.3 = (bf16[128,512]{1,0:T(8,128)(2,1)S(1)}, bf16[128,512]{1,0:T(8,128)(2,1)}, u32[]{:S(2)}) copy-start(bf16[128,512]{1,0:T(8,128)(2,1)} %constant.25.clone.back_ref) | copy-start | bytes 393220
  14.7 46.7 %copy-start.4 = (f32[32,512]{1,0:T(8,128)S(1)}, f32[32,512]{1,0:T(8,128)}, u32[]{:S(2)}) copy-start(f32[32,512]{1,0:T(8,128)} %constant.28.clone.sin_ref) | copy-start | bytes 196612
  14.7 46.7 %copy-start.5 = (f32[32,512]{1,0:T(8,128)S(1)}, f32[32,512]{1,0:T(8,128)}, u32[]{:S(2)}) copy-start(f32[32,512]{1,0:T(8,128)} %constant.27.clone.cos_ref) | copy-start | bytes 196612
  61.4 15.5 %copy-start = (bf16[256,3072]{1,0:T(8,128)(2,1)S(1)}, bf16[256,3072]{1,0:T(8,128)(2,1)}, u32[]{:S(2)}) copy-start(bf16[256,3072]{1,0:T(8,128)(2,1)} %constant.20.clone.table_ref) | copy-start | bytes 4718596
  61.4 15.5 %copy-start.6 = (f32[4,32,128]{2,1,0:T(8,128)S(1)}, f32[4,32,128]{2,1,0:T(8,128)}, u32[]{:S(2)}) copy-start(f32[4,32,128]{2,1,0:T(8,128)} %get-tuple-element.12.tables_ref) | copy-start | bytes 196612
  61.4 15.5 %copy-start.7 = (f32[3072]{0:T(1024)S(1)}, f32[3072]{0:T(1024)}, u32[]{:S(2)}) copy-start(f32[3072]{0:T(1024)} %param.15) | copy-start | bytes 36868

commit v6 on v5

--- a/solution.py
+++ b/solution.py
@@ -204,13 +204,15 @@
 
 
 def subgrid_kernel(
-    recv_ref, kernel_ref, cos_ref, sin_ref, counts_ref, part_ref, back_ref, out_ref,
-    re_ref, im_ref, rows_ref,
+    recv_ref, kernel_ref, cos_ref, sin_ref, counts_hbm, part_ref, back_ref, out_ref,
+    re_ref, im_ref, rows_ref, counts_ref, sem,
 ):
     layers, facets, tall, contrib = recv_ref.shape
     per = tall // 2
     cells = re_ref.shape[1]
     half = facets // 2
+    copy = pltpu.make_async_copy(counts_hbm.at[:, lax.axis_index("layer")], counts_ref, sem)
+    copy.start()
     for f in range(facets // 4):
         first, second, third, fourth = (
             recv_ref[:, n].astype(jnp.float32)
@@ -237,10 +239,15 @@
             else:
                 re_ref[:, span] += re
                 im_ref[:, span] += im
-    counts = lax.dot_general(
-        counts_ref[...].reshape(layers * per, cells).astype(jnp.float32).astype(jnp.bfloat16),
-        part_ref[...], NN, preferred_element_type=jnp.float32,
-    )
+    copy.wait()
+    held = counts_ref[...].astype(jnp.float32).reshape(layers, 2, per, cells // 2)
+    counts = 0.0
+    for n in range(2):
+        counts = counts + lax.dot_general(
+            held[:, n].reshape(layers * per, cells // 2).astype(jnp.bfloat16),
+            part_ref[n * cells // 2 : (n + 1) * cells // 2], NN,
+            preferred_element_type=jnp.float32,
+        )
     weights = jnp.where(counts > 0, 1.0 / jnp.maximum(counts, 1.0), 0.0) * (
         (2 * facets) ** (-0.5)
     )
@@ -318,9 +325,9 @@
     window_row = window.reshape(1, width)
 
     whole = pl.BlockSpec(memory_space=pltpu.VMEM)
-    counts = lax.all_to_all(
-        density.reshape(layers, per, SUB), "layer", split_axis=0, concat_axis=0, tiled=True
-    )
+    counts = density.reshape(layers, per, 2, SUB // 2).transpose(0, 2, 1, 3)
+    counts = counts.reshape(layers, 2 * per, SUB // 2).astype(jnp.bfloat16)
+    counts = lax.all_gather(counts, "layer")
     anywhere = pl.BlockSpec(memory_space=pl.ANY)
     rows = facets * CONTRIB // FINE
     wide = 2 * columns * FINE
@@ -354,7 +361,6 @@
         name="encode",
     )(slabs.reshape(2 * columns, width), window_row, offsets.reshape(1, facets), *folds)
 
-    outgoing, counts = lax.optimization_barrier((outgoing, counts))
     received = lax.all_to_all(
         outgoing.reshape(layers * facets, 2 * per, CONTRIB), ("layer", "facet"),
         split_axis=0, concat_axis=0, tiled=True,
@@ -363,12 +369,14 @@
     back_out = pl.pallas_call(
         subgrid_kernel,
         out_shape=jax.ShapeDtypeStruct((facets, 2 * per, CONTRIB), jnp.bfloat16),
-        in_specs=[whole] * 7,
+        in_specs=[whole] * 4 + [anywhere] + [whole] * 2,
         out_specs=whole,
         scratch_shapes=[
             pltpu.VMEM((columns, SUB), jnp.float32),
             pltpu.VMEM((columns, SUB), jnp.float32),
             pltpu.VMEM((facets * 2 * per, SUB), jnp.bfloat16),
+            pltpu.VMEM((layers, 2 * per, SUB // 2), jnp.bfloat16),
+            pltpu.SemaphoreType.DMA(()),
         ],
         compiler_params=params(48),
         name="subgrid",

time: 79.2 us -> 99.1 us (1.25)
  starting transfers between devices: 6.37 us -> 15.7 us
  blocking collectives: 60.9 us -> 69.3 us
  local copies, waits for them, and re-layouts: 0.05 us -> 2.03 us
    all_to_all x1 -> x0, blocking collectives: 46.6 us -> none  [shards(): lax.all_to_all(outgoing.reshape(layers * facets, 2 * per, CONTRIB), ('lay...]
    all_gather x0 -> x1, blocking collectives: none -> 43.2 us  [shards(): counts = lax.all_gather(counts, 'layer')]
    all_to_all x1, blocking collectives: 14.3 us -> 26.2 us  [shards(): lax.all_to_all(back_out, 'facet', split_axis=0, concat_axis=0, tiled=True)]
    all_to_all x1, starting transfers between devices: 6.37 us -> 15.7 us  [shards(): lax.all_to_all(outgoing.reshape(layers * facets, 2 * per, CONTRIB), ('lay...]
    unnamed x16 -> x18, local copies, waits for them, and re-layouts: 0.05 us -> 2.03 us
  transfers between devices with their start and end apart: 1 -> 1, of which waited for: 0 -> 0; matrix products, arithmetic and copies ran while one was open for 0% -> 0% of each run, Pallas kernels for 10% -> 0%
where the time goes in v6:
time: 99.1 us; the launch traced here: 98.8 us
  blocking collectives  69.3 us (70%)
  starting transfers between devices  15.7 us (16%)
  Pallas kernels  11.6 us (12%)
  local copies, waits for them, and re-layouts  2.03 us (2%)
    all_gather x1, blocking collectives, shards(): counts = lax.all_gather(counts, 'layer')  43.2 us
    all_to_all x1, blocking collectives, shards(): lax.all_to_all(back_out, 'facet', split_axis=0, concat_axis=0, tiled=True)  26.2 us
    all_to_all x1, starting transfers between devices, shards(): lax.all_to_all(outgoing.reshape(layers * facets, 2 * per, CONTRIB), ('lay...  15.7 us
    pallas_call x1, Pallas kernels, shards(): pl.pallas_call(encode_kernel, out_shape=(jax.ShapeDtypeStruct((layers, fa...  8.28 us
    unnamed x18, local copies, waits for them, and re-layouts  2.03 us
    pallas_call x1, Pallas kernels, shards(): pl.pallas_call(decode_kernel, out_shape=jax.ShapeDtypeStruct((2, per, wid...  2 us
  transfers between devices with their start and end apart: 1, of which 0 were waited for; matrix products, arithmetic and copies ran while one was open for 0% of the time, Pallas kernels for 0%

profile of v6, /device:TPU:1, one launch (start us, length us, event | category | flops | bytes accessed | tf_op | source)
XLA Modules:
  0.0 98.8 jit_solution(13545118241369652685)
XLA Ops:
  0.0 8.3 %encode.1 = (bf16[8,32,16,128]{3,2,1,0:T(8,128)(2,1)}, f32[4,32,128]{2,1,0:T(8,128)}) custom-call(bf16[128,3072]{1,0:T(8,128)(2,1)} %bitcast.15, f32[1,3072]{1,0:T(1,128)} %bitcast.11, s32[1,32]{1,0:T(1,128)} %bitcast.16, f32[2,32,1536]{2,1,0:T(8,128)} %constant.21.clone.coarse_hbm, f32[16,1536]{1,0:T(8,128)} %constant.22.clone.fine_hbm, ...), custom_call_target="tpu_custom_call" | custom-call | flops 3221225472 | bytes 12582912 | tf_op jit(solution)/shard_map/encode/pallas_call | solution.py:335
  8.3 0.0 copy-start.8
  8.3 0.0 copy-start.2
  8.3 0.0 copy-start.3
  8.3 0.0 copy-start.5
  8.3 15.7 %all-to-all-start = ((bf16[256,16,128]{2,1,0:T(8,128)(2,1)}), bf16[256,16,128]{2,1,0:T(8,128)(2,1)S(1)}, u32[]{:S(2)}, u32[]{:S(2)}) async-start(bf16[256,16,128]{2,1,0:T(8,128)(2,1)} %bitcast.13), calls=%async_computation | async-start | bytes 2097152 | tf_op jit(solution)/shard_map/all_to_all | solution.py:364
  24.0 0.0 copy-done.8
  24.0 0.0 copy-start.4
  24.0 0.0 copy-start.7
  24.1 43.2 %all_gather.4.counts_hbm = bf16[8,8,16,256]{3,2,1,0:T(8,128)(2,1)S(1)} all-gather(bf16[1,8,16,256]{3,2,1,0:T(8,128)(2,1)S(1)} %bitcast.14), channel_id=1, replica_groups=mesh['layer'=8,'facet'=32] {'layer'}, dimensions={0}, use_global_device_ids=true | all-gather | bytes 589824 | tf_op jit(solution)/shard_map/all_gather | solution.py:330
  67.2 0.0 copy-start
  67.2 0.0 all-to-all-done
  67.2 0.0 copy-done.2
  67.3 0.0 copy-done.3
  67.3 0.0 copy-done.5
  67.3 0.0 copy-start.1
  67.3 1.1 %copy-done.1 = bf16[512,512]{1,0:T(8,128)(2,1)S(1)} copy-done((bf16[512,512]{1,0:T(8,128)(2,1)S(1)}, bf16[512,512]{1,0:T(8,128)(2,1)}, u32[]{:S(2)}) %copy-start.1) | copy-done | bytes 524312
  68.4 0.0 copy-start.6
  68.4 0.8 copy-done.6
  69.3 1.3 %subgrid.1 = bf16[32,16,128]{2,1,0:T(8,128)(2,1)S(1)} custom-call(bf16[8,32,16,128]{3,2,1,0:T(8,128)(2,1)S(1)} %bitcast.10, bf16[128,512]{1,0:T(8,128)(2,1)S(1)} %copy-done.3, f32[32,512]{1,0:T(8,128)S(1)} %copy-done.5, f32[32,512]{1,0:T(8,128)S(1)} %copy-done.6, bf16[8,8,16,256]{3,2,1,0:T(8,128)(2,1)S(1)} %all_gather.4.counts_hbm, ...), custom_call_target="tpu_custom_call" | custom-call | tf_op jit(solution)/shard_map/subgrid/pallas_call | solution.py:369
  70.6 26.2 %all_to_all.10.recv_ref = bf16[32,16,128]{2,1,0:T(8,128)(2,1)S(1)} all-to-all(bf16[32,16,128]{2,1,0:T(8,128)(2,1)S(1)} %subgrid.1), channel_id=1, replica_groups=mesh['layer'=8,'facet'=32] {'facet'}, dimensions={0} | all-to-all | bytes 262144 | tf_op jit(solution)/shard_map/all_to_all | solution.py:385
  96.8 0.0 copy-done.4
  96.8 0.0 copy-done.7
  96.8 0.0 copy-done
  96.8 2.0 %decode.1 = f32[2,8,3072]{2,1,0:T(8,128)} custom-call(bf16[32,16,128]{2,1,0:T(8,128)(2,1)S(1)} %all_to_all.10.recv_ref, f32[1,3072]{1,0:T(1,128)S(1)} %bitcast.12, f32[4,32,128]{2,1,0:T(8,128)S(1)} %copy-done.4, bf16[256,3072]{1,0:T(8,128)(2,1)S(1)} %copy-done), custom_call_target="tpu_custom_call" | custom-call | tf_op jit(solution)/shard_map/decode/pallas_call | solution.py:387
  (1 shorter events, 0.0 us)
Async XLA Ops:
  8.3 15.7 %copy-start.8 = (s32[1,64,512]{2,1,0:T(8,128)S(1)}, s32[1,64,512]{2,1,0:T(8,128)}, u32[]{:S(2)}) copy-start(s32[1,64,512]{2,1,0:T(8,128)} %param.16) | copy-start | bytes 393220
  8.3 59.0 %copy-start.2 = (bf16[128,512]{1,0:T(8,128)(2,1)S(1)}, bf16[128,512]{1,0:T(8,128)(2,1)}, u32[]{:S(2)}) copy-start(bf16[128,512]{1,0:T(8,128)(2,1)} %constant.25.clone.back_ref) | copy-start | bytes 393220
  8.3 58.9 %copy-start.3 = (bf16[128,512]{1,0:T(8,128)(2,1)S(1)}, bf16[128,512]{1,0:T(8,128)(2,1)}, u32[]{:S(2)}) copy-start(bf16[128,512]{1,0:T(8,128)(2,1)} %constant.26.clone.kernel_ref) | copy-start | bytes 393220
  8.3 58.9 %copy-start.5 = (f32[32,512]{1,0:T(8,128)S(1)}, f32[32,512]{1,0:T(8,128)}, u32[]{:S(2)}) copy-start(f32[32,512]{1,0:T(8,128)} %constant.27.clone.cos_ref) | copy-start | bytes 196612
  8.3 58.9 %all-to-all-start = ((bf16[256,16,128]{2,1,0:T(8,128)(2,1)}), bf16[256,16,128]{2,1,0:T(8,128)(2,1)S(1)}, u32[]{:S(2)}, u32[]{:S(2)}) async-start(bf16[256,16,128]{2,1,0:T(8,128)(2,1)} %bitcast.13), calls=%async_computation | async-start | bytes 2097152 | tf_op jit(solution)/shard_map/all_to_all | solution.py:364
  24.0 72.7 %copy-start.4 = (f32[4,32,128]{2,1,0:T(8,128)S(1)}, f32[4,32,128]{2,1,0:T(8,128)}, u32[]{:S(2)}) copy-start(f32[4,32,128]{2,1,0:T(8,128)} %get-tuple-element.8.tables_ref) | copy-start | bytes 196612
  24.0 72.7 %copy-start.7 = (f32[3072]{0:T(1024)S(1)}, f32[3072]{0:T(1024)}, u32[]{:S(2)}) copy-start(f32[3072]{0:T(1024)} %param.15) | copy-start | bytes 36868
  67.2 29.5 %copy-start = (bf16[256,3072]{1,0:T(8,128)(2,1)S(1)}, bf16[256,3072]{1,0:T(8,128)(2,1)}, u32[]{:S(2)}) copy-start(bf16[256,3072]{1,0:T(8,128)(2,1)} %constant.20.clone.table_ref) | copy-start | bytes 4718596
  67.3 1.2 %copy-start.1 = (bf16[512,512]{1,0:T(8,128)(2,1)S(1)}, bf16[512,512]{1,0:T(8,128)(2,1)}, u32[]{:S(2)}) copy-start(bf16[512,512]{1,0:T(8,128)(2,1)} %constant.29.clone.part_ref) | copy-start | bytes 1572868
  68.4 0.8 copy-start.6

commit v7 on v4

--- a/solution.py
+++ b/solution.py
@@ -15,6 +15,7 @@
 FINE = 4
 STEP = 256
 BLOCKS = 2
+SENT = 4
 
 two_pi = 2.0 * math.pi
 NT = (((1,), (1,)), ((), ()))
@@ -86,9 +87,10 @@
 
 
 def encode_kernel(
-    slab_hbm, window_hbm, offsets_ref, coarse_hbm, fine_hbm, turn_hbm, flip_hbm, out_ref, tables_ref,
+    slab_hbm, window_hbm, offsets_ref, coarse_hbm, fine_hbm, turn_hbm, flip_hbm, out_hbm, cells_hbm,
     slab_ref, window_ref, coarse_ref, fine_ref, turn_ref, flip_ref,
-    phase_ref, side_ref, turn_table_ref, wave_ref, total_ref, sems,
+    phase_ref, side_ref, turn_table_ref, wave_ref, total_ref,
+    out_ref, cells_ref, sems, out_sems,
 ):
     columns = slab_ref.shape[0] // 2
     width = slab_ref.shape[1]
@@ -103,9 +105,14 @@
     for copy in copies:
         copy.start()
     turns = offset_tables(offsets_ref, lax.axis_index("facet"), width)
-    for n in range(2):
-        tables_ref[n] = turns["start"][n]
-        tables_ref[2 + n] = turns["cell"][n]
+    (cos_a, sin_a), (cos_b, sin_b) = turns["start"], turns["cell"]
+    for tile in range(width // LANES):
+        c, s = cos_a[:, tile : tile + 1], sin_a[:, tile : tile + 1]
+        span = slice(tile * LANES, (tile + 1) * LANES)
+        cells_ref[0, :, span] = c * cos_b - s * sin_b
+        cells_ref[1, :, span] = s * cos_b + c * sin_b
+    leaving = [pltpu.make_async_copy(cells_ref, cells_hbm, out_sems.at[subgrids // SENT])]
+    leaving[0].start()
     high, low, centre = turns["tile"], turns["inner"], turns["middle"]
     for tile in range(half // LANES):
         c, s = high[0][:, tile : tile + 1], high[1][:, tile : tile + 1]
@@ -168,7 +175,7 @@
         for fine in range(FINE):
             block = total_ref[s * rows : (s + 1) * rows, fine * LANES : (fine + 1) * LANES]
             blocks.append(block * c + pltpu.roll(block, columns, 1) * d)
-        out_ref[s] = jnp.concatenate(blocks, 0).T.astype(jnp.bfloat16)
+        out_ref[s] = jnp.concatenate(blocks, 0).astype(jnp.bfloat16).T
 
     steps = half // STEP
     each = subgrids // BLOCKS
@@ -195,6 +202,15 @@
             else:
                 for s in range(block * each, (block + 1) * each):
                     finish(s)
+                    if s % SENT == SENT - 1:
+                        done = slice(s + 1 - SENT, s + 1)
+                        copy = pltpu.make_async_copy(
+                            out_ref.at[done], out_hbm.at[done], out_sems.at[s // SENT]
+                        )
+                        copy.start()
+                        leaving.append(copy)
+    for copy in leaving:
+        copy.wait()
 
 
 def grid_kernel(
@@ -260,16 +276,11 @@
 
 
 def decode_kernel(
-    recv_ref, window_ref, tables_ref, table_ref, out_ref, pr_ref, pi_ref
+    recv_ref, window_ref, phases_ref, table_ref, out_ref
 ):
     subgrids = recv_ref.shape[0]
     per = recv_ref.shape[1] // 2
     width = out_ref.shape[2]
-    for tile in range(width // LANES):
-        c, s = tables_ref[0, :, tile : tile + 1], tables_ref[1, :, tile : tile + 1]
-        span = slice(tile * LANES, (tile + 1) * LANES)
-        pr_ref[:, span] = c * tables_ref[2] - s * tables_ref[3]
-        pi_ref[:, span] = s * tables_ref[2] + c * tables_ref[3]
     rows = recv_ref[...].astype(jnp.float32)
     re, im = rows[:, :per], rows[:, per:]
     left_re = jnp.concatenate([re, im], 2).reshape(subgrids * per, 2 * CONTRIB).astype(jnp.bfloat16)
@@ -284,8 +295,8 @@
         for s in range(subgrids):
             a = zr[s * per : (s + 1) * per]
             b = zi[s * per : (s + 1) * per]
-            pr = pr_ref[s : s + 1, span]
-            pi = pi_ref[s : s + 1, span]
+            pr = phases_ref[0, s : s + 1, span]
+            pi = phases_ref[1, s : s + 1, span]
             re_term = pr * a - pi * b
             im_term = pr * b + pi * a
             out_re = re_term if out_re is None else out_re + re_term
@@ -325,14 +336,14 @@
     rows = facets * CONTRIB // FINE
     wide = 2 * columns * FINE
     half = width // 2
-    outgoing, tables = pl.pallas_call(
+    outgoing, cell_phases = pl.pallas_call(
         encode_kernel,
         out_shape=(
             jax.ShapeDtypeStruct((facets, 2 * columns, CONTRIB), jnp.bfloat16),
-            jax.ShapeDtypeStruct((4, facets, LANES), jnp.float32),
+            jax.ShapeDtypeStruct((2, facets, width), jnp.float32),
         ),
         in_specs=[anywhere, anywhere, whole] + [anywhere] * 4,
-        out_specs=(whole, whole),
+        out_specs=(anywhere, anywhere),
         scratch_shapes=[
             pltpu.VMEM((2 * columns, width), jnp.bfloat16),
             pltpu.VMEM((1, width), jnp.float32),
@@ -345,7 +356,10 @@
             pltpu.VMEM((2, rows, 2 * STEP), jnp.bfloat16),
             pltpu.VMEM((2, wide, 2 * STEP), jnp.bfloat16),
             pltpu.VMEM((rows, wide), jnp.float32),
+            pltpu.VMEM((facets, 2 * columns, CONTRIB), jnp.bfloat16),
+            pltpu.VMEM((2, facets, width), jnp.float32),
             pltpu.SemaphoreType.DMA((6,)),
+            pltpu.SemaphoreType.DMA((facets // SENT + 1,)),
         ],
         compiler_params=params(60),
         name="encode",
@@ -382,10 +396,9 @@
         out_shape=jax.ShapeDtypeStruct((2, per, width), jnp.float32),
         in_specs=[whole] * 4,
         out_specs=whole,
-        scratch_shapes=[pltpu.VMEM((facets, width), jnp.float32)] * 2,
         compiler_params=params(48),
         name="decode",
-    )(returned, window_row, tables, table)
+    )(returned, window_row, cell_phases, table)
 
 
 def solution(mesh):

time: 79.9 us -> 79.1 us (0.990)
  Pallas kernels: 11.5 us -> 10.7 us
where the time goes in v7:
time: 79.1 us; the launch traced here: 78.8 us
  blocking collectives  68 us (86%)
  Pallas kernels  10.7 us (14%)
    all_to_all x1, blocking collectives, shards(): lax.all_to_all(outgoing, 'facet', split_axis=0, concat_axis=0, tiled=True)  40.6 us
    all_to_all x1, blocking collectives, shards(): lax.all_to_all(back_out, 'facet', split_axis=0, concat_axis=0, tiled=True)  16.1 us
    all_to_all x1, blocking collectives, shards(): lax.all_to_all(gridded, 'layer', split_axis=0, concat_axis=0, tiled=True)  11.2 us
    pallas_call x1, Pallas kernels, shards(): pl.pallas_call(encode_kernel, out_shape=(jax.ShapeDtypeStruct((facets, 2...  7.79 us
    pallas_call x1, Pallas kernels, shards(): pl.pallas_call(decode_kernel, out_shape=jax.ShapeDtypeStruct((2, per, wid...  1.76 us

profile of v7, /device:TPU:1, one launch (start us, length us, event | category | flops | bytes accessed | tf_op | source)
XLA Modules:
  0.0 78.8 jit_solution(16561251843704890030)
XLA Ops:
  0.0 0.0 copy-start.2
  0.0 0.0 copy-start.3
  0.0 0.0 copy-start.4
  0.0 0.0 copy-start.5
  0.0 0.0 copy-start.6
  0.0 7.8 %encode.1 = (bf16[32,128,128]{2,1,0:T(8,128)(2,1)}, f32[2,32,3072]{2,1,0:T(8,128)}) custom-call(bf16[128,3072]{1,0:T(8,128)(2,1)} %bitcast.7, f32[1,3072]{1,0:T(1,128)} %bitcast.5, s32[1,32]{1,0:T(1,128)} %bitcast.8, f32[2,32,1536]{2,1,0:T(8,128)} %constant.21.clone.coarse_hbm, f32[16,1536]{1,0:T(8,128)} %constant.22.clone.fine_hbm, ...), custom_call_target="tpu_custom_call" | custom-call | tf_op jit(solution)/shard_map/encode/pallas_call | solution.py:339
  7.8 40.6 %all_to_all.15.recv_ref = bf16[32,128,128]{2,1,0:T(8,128)(2,1)S(1)} all-to-all(bf16[32,128,128]{2,1,0:T(8,128)(2,1)} %get-tuple-element.7), channel_id=1, replica_groups=mesh['layer'=8,'facet'=32] {'facet'}, dimensions={0} | all-to-all | bytes 2097152 | tf_op jit(solution)/shard_map/all_to_all | solution.py:368
  48.5 0.0 copy-start.7
  48.5 0.0 copy-done.2
  48.5 0.0 copy-done.3
  48.5 0.0 copy-done.4
  48.5 0.0 copy-done.5
  48.5 0.0 copy-done.6
  48.5 0.0 copy-start
  48.5 0.0 copy-start.1
  48.5 0.0 copy-start.8
  48.5 0.9 %subgrid.1 = bf16[8,16,512]{2,1,0:T(8,128)(2,1)S(1)} custom-call(bf16[32,128,128]{2,1,0:T(8,128)(2,1)S(1)} %all_to_all.15.recv_ref, bf16[128,512]{1,0:T(8,128)(2,1)S(1)} %copy-done.6, f32[32,512]{1,0:T(8,128)S(1)} %copy-done.4, f32[32,512]{1,0:T(8,128)S(1)} %copy-done.3, s32[64,512]{1,0:T(8,128)S(1)} %bitcast.4, bf16[512,512]{1,0:T(8,128)(2,1)S(1)} %copy-done.2), custom_call_target="tpu_custom_call" | custom-call | tf_op jit(solution)/shard_map/subgrid/pallas_call | solution.py:370
  49.4 11.2 %all_to_all.16.recv_ref = bf16[8,16,512]{2,1,0:T(8,128)(2,1)S(1)} all-to-all(bf16[8,16,512]{2,1,0:T(8,128)(2,1)S(1)} %subgrid.1), channel_id=1, replica_groups=mesh['layer'=8,'facet'=32] {'layer'}, dimensions={0} | all-to-all | bytes 262144 | tf_op jit(solution)/shard_map/all_to_all | solution.py:380
  60.6 0.0 copy-done.7
  60.6 0.3 back.1
  61.0 16.1 %all_to_all.17.recv_ref = bf16[32,16,128]{2,1,0:T(8,128)(2,1)S(1)} all-to-all(bf16[32,16,128]{2,1,0:T(8,128)(2,1)S(1)} %back.1), channel_id=1, replica_groups=mesh['layer'=8,'facet'=32] {'facet'}, dimensions={0} | all-to-all | bytes 262144 | tf_op jit(solution)/shard_map/all_to_all | solution.py:392
  77.1 0.0 copy-done
  77.1 0.0 copy-done.1
  77.1 0.0 copy-done.8
  77.1 1.8 %decode.1 = f32[2,8,3072]{2,1,0:T(8,128)} custom-call(bf16[32,16,128]{2,1,0:T(8,128)(2,1)S(1)} %all_to_all.17.recv_ref, f32[1,3072]{1,0:T(1,128)S(1)} %bitcast.6, f32[2,32,3072]{2,1,0:T(8,128)S(1)} %copy-done.1, bf16[256,3072]{1,0:T(8,128)(2,1)S(1)} %copy-done), custom_call_target="tpu_custom_call" | custom-call | tf_op jit(solution)/shard_map/decode/pallas_call | solution.py:394
Async XLA Ops:
  0.0 48.5 %copy-start.2 = (bf16[512,512]{1,0:T(8,128)(2,1)S(1)}, bf16[512,512]{1,0:T(8,128)(2,1)}, u32[]{:S(2)}) copy-start(bf16[512,512]{1,0:T(8,128)(2,1)} %constant.29.clone.part_ref) | copy-start | bytes 1572868
  0.0 48.5 %copy-start.3 = (f32[32,512]{1,0:T(8,128)S(1)}, f32[32,512]{1,0:T(8,128)}, u32[]{:S(2)}) copy-start(f32[32,512]{1,0:T(8,128)} %constant.28.clone.sin_ref) | copy-start | bytes 196612
  0.0 48.5 %copy-start.4 = (f32[32,512]{1,0:T(8,128)S(1)}, f32[32,512]{1,0:T(8,128)}, u32[]{:S(2)}) copy-start(f32[32,512]{1,0:T(8,128)} %constant.27.clone.cos_ref) | copy-start | bytes 196612
  0.0 48.5 %copy-start.5 = (s32[1,64,512]{2,1,0:T(8,128)S(1)}, s32[1,64,512]{2,1,0:T(8,128)}, u32[]{:S(2)}) copy-start(s32[1,64,512]{2,1,0:T(8,128)} %param.16) | copy-start | bytes 393220
  0.0 48.5 %copy-start.6 = (bf16[128,512]{1,0:T(8,128)(2,1)S(1)}, bf16[128,512]{1,0:T(8,128)(2,1)}, u32[]{:S(2)}) copy-start(bf16[128,512]{1,0:T(8,128)(2,1)} %constant.26.clone.kernel_ref) | copy-start | bytes 393220
  48.5 12.2 %copy-start.7 = (bf16[128,512]{1,0:T(8,128)(2,1)S(1)}, bf16[128,512]{1,0:T(8,128)(2,1)}, u32[]{:S(2)}) copy-start(bf16[128,512]{1,0:T(8,128)(2,1)} %constant.25.clone.kernel_ref) | copy-start | bytes 393220
  48.5 28.6 %copy-start = (bf16[256,3072]{1,0:T(8,128)(2,1)S(1)}, bf16[256,3072]{1,0:T(8,128)(2,1)}, u32[]{:S(2)}) copy-start(bf16[256,3072]{1,0:T(8,128)(2,1)} %constant.20.clone.table_ref) | copy-start | bytes 4718596
  48.5 28.6 %copy-start.1 = (f32[2,32,3072]{2,1,0:T(8,128)S(1)}, f32[2,32,3072]{2,1,0:T(8,128)}, u32[]{:S(2)}) copy-start(f32[2,32,3072]{2,1,0:T(8,128)} %get-tuple-element.8.phases_ref) | copy-start | bytes 2359300
  48.5 28.5 %copy-start.8 = (f32[3072]{0:T(1024)S(1)}, f32[3072]{0:T(1024)}, u32[]{:S(2)}) copy-start(f32[3072]{0:T(1024)} %param.15) | copy-start | bytes 36868

commit v8 on v7

--- a/solution.py
+++ b/solution.py
@@ -361,7 +361,7 @@
             pltpu.SemaphoreType.DMA((6,)),
             pltpu.SemaphoreType.DMA((facets // SENT + 1,)),
         ],
-        compiler_params=params(60),
+        compiler_params=params(24),
         name="encode",
     )(slabs.reshape(2 * columns, width), window_row, offsets.reshape(1, facets), *folds)
 

time: 79.1 us -> 86.7 us (1.096)
  local copies, waits for them, and re-layouts: 0.04 us -> 6.08 us
  Pallas kernels: 10.7 us -> 12.4 us
    unnamed x18 -> x30, local copies, waits for them, and re-layouts: 0.04 us -> 6.08 us
    pallas_call x1, Pallas kernels: 7.79 us -> 9.5 us  [shards(): pl.pallas_call(encode_kernel, out_shape=(jax.ShapeDtypeStruct((facets, 2...]
    all_to_all x1, blocking collectives: 11.2 us -> 10.2 us  [shards(): lax.all_to_all(gridded, 'layer', split_axis=0, concat_axis=0, tiled=True)]
where the time goes in v8:
time: 86.7 us; the launch traced here: 86.3 us
  blocking collectives  67.7 us (78%)
  Pallas kernels  12.4 us (14%)
  local copies, waits for them, and re-layouts  6.08 us (7%)
    all_to_all x1, blocking collectives, shards(): lax.all_to_all(outgoing, 'facet', split_axis=0, concat_axis=0, tiled=True)  41.3 us
    all_to_all x1, blocking collectives, shards(): lax.all_to_all(back_out, 'facet', split_axis=0, concat_axis=0, tiled=True)  16.2 us
    all_to_all x1, blocking collectives, shards(): lax.all_to_all(gridded, 'layer', split_axis=0, concat_axis=0, tiled=True)  10.2 us
    pallas_call x1, Pallas kernels, shards(): pl.pallas_call(encode_kernel, out_shape=(jax.ShapeDtypeStruct((facets, 2...  9.5 us
    unnamed x30, local copies, waits for them, and re-layouts  6.08 us
    pallas_call x1, Pallas kernels, shards(): pl.pallas_call(decode_kernel, out_shape=jax.ShapeDtypeStruct((2, per, wid...  1.76 us

profile of v8, /device:TPU:1, one launch (start us, length us, event | category | flops | bytes accessed | tf_op | source)
XLA Modules:
  0.0 86.3 jit_solution(4448544708693990864)
XLA Ops:
  0.0 0.0 copy-start.1
  0.0 1.1 %copy-done.1 = bf16[1,2,64,3072]{3,2,1,0:T(8,128)(2,1)S(1)} copy-done((bf16[1,2,64,3072]{3,2,1,0:T(8,128)(2,1)S(1)}, bf16[1,2,64,3072]{3,2,1,0:T(8,128)(2,1)}, u32[]{:S(2)}) %copy-start.1) | copy-done | bytes 786456
  1.1 0.0 copy-start.3
  1.1 1.0 %copy-done.3 = f32[2,32,1536]{2,1,0:T(8,128)S(1)} copy-done((f32[2,32,1536]{2,1,0:T(8,128)S(1)}, f32[2,32,1536]{2,1,0:T(8,128)}, u32[]{:S(2)}) %copy-start.3) | copy-done | bytes 393240
  2.1 0.0 copy-start.9
  2.1 0.9 %copy-done.9 = bf16[256,256]{1,0:T(8,128)(2,1)S(1)} copy-done((bf16[256,256]{1,0:T(8,128)(2,1)S(1)}, bf16[256,256]{1,0:T(8,128)(2,1)}, u32[]{:S(2)}) %copy-start.9) | copy-done | bytes 131096
  3.0 0.0 copy-start.10
  3.0 0.9 %copy-done.10 = f32[16,1536]{1,0:T(8,128)S(1)} copy-done((f32[16,1536]{1,0:T(8,128)S(1)}, f32[16,1536]{1,0:T(8,128)}, u32[]{:S(2)}) %copy-start.10) | copy-done | bytes 98328
  3.9 0.0 copy-start.11
  3.9 0.7 copy-done.11
  4.6 0.0 copy-start.13
  4.6 0.8 copy-done.13
  5.4 0.0 copy-start.14
  5.4 0.7 copy-done.14
  6.0 0.0 copy-start.2
  6.1 0.0 copy-start.4
  6.1 0.0 copy-start.5
  6.1 0.0 copy-start.6
  6.1 0.0 copy-start.7
  6.1 9.5 %encode.1 = (bf16[32,128,128]{2,1,0:T(8,128)(2,1)S(1)}, f32[2,32,3072]{2,1,0:T(8,128)S(1)}) custom-call(bf16[128,3072]{1,0:T(8,128)(2,1)S(1)} %bitcast.4, f32[1,3072]{1,0:T(1,128)S(1)} %bitcast.6, s32[1,32]{1,0:T(1,128)S(1)} %bitcast.8, f32[2,32,1536]{2,1,0:T(8,128)S(1)} %copy-done.3, f32[16,1536]{1,0:T(8,128)S(1)} %copy-done.10, ...), custom_call_target="tpu_custom_call" | custom-call | tf_op jit(solution)/shard_map/encode/pallas_call | solution.py:339
  15.6 41.3 %all_to_all.15.recv_ref = bf16[32,128,128]{2,1,0:T(8,128)(2,1)S(1)} all-to-all(bf16[32,128,128]{2,1,0:T(8,128)(2,1)S(1)} %get-tuple-element.7), channel_id=1, replica_groups=mesh['layer'=8,'facet'=32] {'facet'}, dimensions={0} | all-to-all | bytes 2097152 | tf_op jit(solution)/shard_map/all_to_all | solution.py:368
  56.9 0.0 copy-start.8
  56.9 0.0 copy-done.2
  56.9 0.0 copy-done.4
  56.9 0.0 copy-done.5
  56.9 0.0 copy-done.6
  56.9 0.0 copy-done.7
  56.9 0.0 copy-start
  56.9 0.0 copy-start.12
  56.9 0.9 %subgrid.1 = bf16[8,16,512]{2,1,0:T(8,128)(2,1)S(1)} custom-call(bf16[32,128,128]{2,1,0:T(8,128)(2,1)S(1)} %all_to_all.15.recv_ref, bf16[128,512]{1,0:T(8,128)(2,1)S(1)} %copy-done.7, f32[32,512]{1,0:T(8,128)S(1)} %copy-done.5, f32[32,512]{1,0:T(8,128)S(1)} %copy-done.4, s32[64,512]{1,0:T(8,128)S(1)} %bitcast.5, bf16[512,512]{1,0:T(8,128)(2,1)S(1)} %copy-done.2), custom_call_target="tpu_custom_call" | custom-call | tf_op jit(solution)/shard_map/subgrid/pallas_call | solution.py:370
  57.8 10.2 %all_to_all.16.recv_ref = bf16[8,16,512]{2,1,0:T(8,128)(2,1)S(1)} all-to-all(bf16[8,16,512]{2,1,0:T(8,128)(2,1)S(1)} %subgrid.1), channel_id=1, replica_groups=mesh['layer'=8,'facet'=32] {'layer'}, dimensions={0} | all-to-all | bytes 262144 | tf_op jit(solution)/shard_map/all_to_all | solution.py:380
  68.0 0.0 copy-done.8
  68.0 0.3 back.1
  68.4 16.2 %all_to_all.17.recv_ref = bf16[32,16,128]{2,1,0:T(8,128)(2,1)S(1)} all-to-all(bf16[32,16,128]{2,1,0:T(8,128)(2,1)S(1)} %back.1), channel_id=1, replica_groups=mesh['layer'=8,'facet'=32] {'facet'}, dimensions={0} | all-to-all | bytes 262144 | tf_op jit(solution)/shard_map/all_to_all | solution.py:392
  84.5 0.0 copy-done
  84.5 0.0 copy-done.12
  84.5 1.8 %decode.1 = f32[2,8,3072]{2,1,0:T(8,128)} custom-call(bf16[32,16,128]{2,1,0:T(8,128)(2,1)S(1)} %all_to_all.17.recv_ref, f32[1,3072]{1,0:T(1,128)S(1)} %bitcast.7, f32[2,32,3072]{2,1,0:T(8,128)S(1)} %get-tuple-element.8.phases_ref, bf16[256,3072]{1,0:T(8,128)(2,1)S(1)} %copy-done), custom_call_target="tpu_custom_call" | custom-call | tf_op jit(solution)/shard_map/decode/pallas_call | solution.py:394
Async XLA Ops:
  0.0 1.1 %copy-start.1 = (bf16[1,2,64,3072]{3,2,1,0:T(8,128)(2,1)S(1)}, bf16[1,2,64,3072]{3,2,1,0:T(8,128)(2,1)}, u32[]{:S(2)}) copy-start(bf16[1,2,64,3072]{3,2,1,0:T(8,128)(2,1)} %param.14) | copy-start | bytes 2359300
  1.1 1.0 %copy-start.3 = (f32[2,32,1536]{2,1,0:T(8,128)S(1)}, f32[2,32,1536]{2,1,0:T(8,128)}, u32[]{:S(2)}) copy-start(f32[2,32,1536]{2,1,0:T(8,128)} %constant.21.clone.coarse_hbm) | copy-start | bytes 1179652
  2.1 0.9 %copy-start.9 = (bf16[256,256]{1,0:T(8,128)(2,1)S(1)}, bf16[256,256]{1,0:T(8,128)(2,1)}, u32[]{:S(2)}) copy-start(bf16[256,256]{1,0:T(8,128)(2,1)} %constant.24.clone.flip_hbm) | copy-start | bytes 393220
  3.0 0.9 %copy-start.10 = (f32[16,1536]{1,0:T(8,128)S(1)}, f32[16,1536]{1,0:T(8,128)}, u32[]{:S(2)}) copy-start(f32[16,1536]{1,0:T(8,128)} %constant.22.clone.fine_hbm) | copy-start | bytes 294916
  3.9 0.7 copy-start.11
  4.6 0.8 copy-start.13
  5.4 0.7 copy-start.14
  6.0 50.8 %copy-start.2 = (bf16[512,512]{1,0:T(8,128)(2,1)S(1)}, bf16[512,512]{1,0:T(8,128)(2,1)}, u32[]{:S(2)}) copy-start(bf16[512,512]{1,0:T(8,128)(2,1)} %constant.29.clone.part_ref) | copy-start | bytes 1572868
  6.1 50.8 %copy-start.4 = (f32[32,512]{1,0:T(8,128)S(1)}, f32[32,512]{1,0:T(8,128)}, u32[]{:S(2)}) copy-start(f32[32,512]{1,0:T(8,128)} %constant.28.clone.sin_ref) | copy-start | bytes 196612
  6.1 50.8 %copy-start.5 = (f32[32,512]{1,0:T(8,128)S(1)}, f32[32,512]{1,0:T(8,128)}, u32[]{:S(2)}) copy-start(f32[32,512]{1,0:T(8,128)} %constant.27.clone.cos_ref) | copy-start | bytes 196612
  6.1 50.8 %copy-start.6 = (s32[1,64,512]{2,1,0:T(8,128)S(1)}, s32[1,64,512]{2,1,0:T(8,128)}, u32[]{:S(2)}) copy-start(s32[1,64,512]{2,1,0:T(8,128)} %param.16) | copy-start | bytes 393220
  6.1 50.8 %copy-start.7 = (bf16[128,512]{1,0:T(8,128)(2,1)S(1)}, bf16[128,512]{1,0:T(8,128)(2,1)}, u32[]{:S(2)}) copy-start(bf16[128,512]{1,0:T(8,128)(2,1)} %constant.26.clone.kernel_ref) | copy-start | bytes 393220
  56.9 11.2 %copy-start.8 = (bf16[128,512]{1,0:T(8,128)(2,1)S(1)}, bf16[128,512]{1,0:T(8,128)(2,1)}, u32[]{:S(2)}) copy-start(bf16[128,512]{1,0:T(8,128)(2,1)} %constant.25.clone.kernel_ref) | copy-start | bytes 393220
  56.9 27.6 %copy-start = (bf16[256,3072]{1,0:T(8,128)(2,1)S(1)}, bf16[256,3072]{1,0:T(8,128)(2,1)}, u32[]{:S(2)}) copy-start(bf16[256,3072]{1,0:T(8,128)(2,1)} %constant.20.clone.table_ref) | copy-start | bytes 4718596
  56.9 27.6 %copy-start.12 = (f32[3072]{0:T(1024)S(1)}, f32[3072]{0:T(1024)}, u32[]{:S(2)}) copy-start(f32[3072]{0:T(1024)} %param.15) | copy-start | bytes 36868

commit v9 on v7

--- a/solution.py
+++ b/solution.py
@@ -373,7 +373,7 @@
         in_specs=[whole] * 6,
         out_specs=whole,
         scratch_shapes=[pltpu.VMEM((columns, SUB), jnp.float32)] * 2,
-        compiler_params=params(48),
+        compiler_params=params(60),
         name="subgrid",
     )(received, spread_in, cos_u, sin_u, density[0], jnp.asarray(parting))
 
@@ -385,7 +385,7 @@
         in_specs=[whole] * 4,
         out_specs=whole,
         scratch_shapes=[pltpu.VMEM((facets * 2 * per, SUB), jnp.bfloat16)],
-        compiler_params=params(48),
+        compiler_params=params(60),
         name="back",
     )(by_layer, spread, cos_u, sin_u)
 
@@ -396,7 +396,7 @@
         out_shape=jax.ShapeDtypeStruct((2, per, width), jnp.float32),
         in_specs=[whole] * 4,
         out_specs=whole,
-        compiler_params=params(48),
+        compiler_params=params(60),
         name="decode",
     )(returned, window_row, cell_phases, table)
 

time: 79.1 us -> 86.2 us (1.090)
  Pallas kernels: 10.7 us -> 16.2 us
  blocking collectives: 68 us -> 69.5 us
    pallas_call x1, Pallas kernels: 0.86 us -> 3.06 us  [shards(): pl.pallas_call(grid_kernel, out_shape=jax.ShapeDtypeStruct((layers, 2 * p...]
    pallas_call x1, Pallas kernels: 1.76 us -> 3.49 us  [shards(): pl.pallas_call(decode_kernel, out_shape=jax.ShapeDtypeStruct((2, per, wid...]
    pallas_call x1, Pallas kernels: 0.31 us -> 1.96 us  [shards(): pl.pallas_call(back_kernel, out_shape=jax.ShapeDtypeStruct((facets, 2 * p...]
    all_to_all x1, blocking collectives: 16.1 us -> 17.2 us  [shards(): lax.all_to_all(back_out, 'facet', split_axis=0, concat_axis=0, tiled=True)]
    all_to_all x1, blocking collectives: 40.6 us -> 41.6 us  [shards(): lax.all_to_all(outgoing, 'facet', split_axis=0, concat_axis=0, tiled=True)]
where the time goes in v9:
time: 86.2 us; the launch traced here: 85.8 us
  blocking collectives  69.5 us (81%)
  Pallas kernels  16.2 us (19%)
    all_to_all x1, blocking collectives, shards(): lax.all_to_all(outgoing, 'facet', split_axis=0, concat_axis=0, tiled=True)  41.6 us
    all_to_all x1, blocking collectives, shards(): lax.all_to_all(back_out, 'facet', split_axis=0, concat_axis=0, tiled=True)  17.2 us
    all_to_all x1, blocking collectives, shards(): lax.all_to_all(gridded, 'layer', split_axis=0, concat_axis=0, tiled=True)  10.7 us
    pallas_call x1, Pallas kernels, shards(): pl.pallas_call(encode_kernel, out_shape=(jax.ShapeDtypeStruct((facets, 2...  7.74 us
    pallas_call x1, Pallas kernels, shards(): pl.pallas_call(decode_kernel, out_shape=jax.ShapeDtypeStruct((2, per, wid...  3.49 us
    pallas_call x1, Pallas kernels, shards(): pl.pallas_call(grid_kernel, out_shape=jax.ShapeDtypeStruct((layers, 2 * p...  3.06 us
    pallas_call x1, Pallas kernels, shards(): pl.pallas_call(back_kernel, out_shape=jax.ShapeDtypeStruct((facets, 2 * p...  1.96 us

profile of v9, /device:TPU:1, one launch (start us, length us, event | category | flops | bytes accessed | tf_op | source)
XLA Modules:
  0.0 85.8 jit_solution(12381065059824245649)
XLA Ops:
  0.0 7.7 %encode.1 = (bf16[32,128,128]{2,1,0:T(8,128)(2,1)}, f32[2,32,3072]{2,1,0:T(8,128)}) custom-call(bf16[128,3072]{1,0:T(8,128)(2,1)} %bitcast.4, f32[1,3072]{1,0:T(1,128)} %bitcast.6, s32[1,32]{1,0:T(1,128)} %bitcast.8, f32[2,32,1536]{2,1,0:T(8,128)} %constant.21.clone.coarse_hbm, f32[16,1536]{1,0:T(8,128)} %constant.22.clone.fine_hbm, ...), custom_call_target="tpu_custom_call" | custom-call | tf_op jit(solution)/shard_map/encode/pallas_call | solution.py:339
  7.7 41.6 %all_to_all.15.recv_ref = bf16[32,128,128]{2,1,0:T(8,128)(2,1)} all-to-all(bf16[32,128,128]{2,1,0:T(8,128)(2,1)} %get-tuple-element.7), channel_id=1, replica_groups=mesh['layer'=8,'facet'=32] {'facet'}, dimensions={0} | all-to-all | bytes 2097152 | tf_op jit(solution)/shard_map/all_to_all | solution.py:368
  49.4 3.1 %subgrid.1 = bf16[8,16,512]{2,1,0:T(8,128)(2,1)} custom-call(bf16[32,128,128]{2,1,0:T(8,128)(2,1)} %all_to_all.15.recv_ref, bf16[128,512]{1,0:T(8,128)(2,1)} %constant.26.clone.kernel_ref, f32[32,512]{1,0:T(8,128)} %constant.27.clone.cos_ref, f32[32,512]{1,0:T(8,128)} %constant.28.clone.sin_ref, s32[64,512]{1,0:T(8,128)} %bitcast.5, ...), custom_call_target="tpu_custom_call" | custom-call | tf_op jit(solution)/shard_map/subgrid/pallas_call | solution.py:370
  52.4 10.7 %all_to_all.16.recv_ref = bf16[8,16,512]{2,1,0:T(8,128)(2,1)} all-to-all(bf16[8,16,512]{2,1,0:T(8,128)(2,1)} %subgrid.1), channel_id=1, replica_groups=mesh['layer'=8,'facet'=32] {'layer'}, dimensions={0} | all-to-all | bytes 262144 | tf_op jit(solution)/shard_map/all_to_all | solution.py:380
  63.1 2.0 %back.1 = bf16[32,16,128]{2,1,0:T(8,128)(2,1)} custom-call(bf16[8,16,512]{2,1,0:T(8,128)(2,1)} %all_to_all.16.recv_ref, bf16[128,512]{1,0:T(8,128)(2,1)} %constant.25.clone.kernel_ref, f32[32,512]{1,0:T(8,128)} %constant.27.clone.cos_ref, f32[32,512]{1,0:T(8,128)} %constant.28.clone.sin_ref), custom_call_target="tpu_custom_call" | custom-call | tf_op jit(solution)/shard_map/back/pallas_call | solution.py:382
  65.1 17.2 %all_to_all.17.recv_ref = bf16[32,16,128]{2,1,0:T(8,128)(2,1)} all-to-all(bf16[32,16,128]{2,1,0:T(8,128)(2,1)} %back.1), channel_id=1, replica_groups=mesh['layer'=8,'facet'=32] {'facet'}, dimensions={0} | all-to-all | bytes 262144 | tf_op jit(solution)/shard_map/all_to_all | solution.py:392
  82.3 3.5 %decode.1 = f32[2,8,3072]{2,1,0:T(8,128)} custom-call(bf16[32,16,128]{2,1,0:T(8,128)(2,1)} %all_to_all.17.recv_ref, f32[1,3072]{1,0:T(1,128)} %bitcast.7, f32[2,32,3072]{2,1,0:T(8,128)} %get-tuple-element.8.phases_ref, bf16[256,3072]{1,0:T(8,128)(2,1)} %constant.20.clone.table_ref), custom_call_target="tpu_custom_call" | custom-call | tf_op jit(solution)/shard_map/decode/pallas_call | solution.py:394
